TPU v7x, 128 devices: a whole 4x4x4 slice. The times are simulated.
128 devices in a mesh: az: 16 (over z_hi, x, core), rad: 8 (over z_lo, y).
Axes of the slice: x: 4, y: 4, z: 4 (z_hi: 2, z_lo: 2; z = z_hi * 2 + z_lo), core: 2. Of those that a mesh axis runs over, the one named last changes fastest.
Arguments:
- conserved: float32 [5, 16, 128, 4096], P(None, None, 'rad', 'az'), as said below
- shift_cells: int32 [128], P('rad'), may hold values from 0 to 4095, as said below
- shift_frac: float32 [128], P('rad'), may hold values from 0 to 1
- boundary_offset: int32 [1], replicated, may hold values from 0 to 4095
Outputs:
- advected: float32 [5, 16, 128, 4096], P(None, None, 'rad', 'az')
Inputs may be any that keep to these rules, and one draw needn't show every extreme that they name: The density and pressure of conserved lie between 0.5 and 2 and each velocity component is at most 0.8 in magnitude. `shift_cells`: both 0 and 4095 occur in every draw.
All inputs are finite; a program needn't handle non-finite values.
Results may differ from a plain program's by a relative error of at most 0.0003.
Values sent between devices are 32-bit elements; how exact they have to be, the bound alone decides.
No kernel may reach another device: no remote copies, remote signals or barrier semaphores. Data moves between devices by JAX's collectives and lax.ppermute only.
A program may use at most 448 MiB of HBM per device.

v0:
```python
import functools

import jax
import jax.numpy as jnp
from jax import lax
from jax.experimental import pallas as pl
from jax.experimental.pallas import tpu as pltpu
from jax.sharding import PartitionSpec as P

gamma_ratio = 5.0 / 3.0
step_ratio = 0.06
omega_rate = 1.0
shear_rate = 1.5

NZ = 16
NROW = 16
NC = 256
LANES = 128
WIDTH = 3
NFULL = NROW + 2 * WIDTH
GROUP = 8
VMEM = pl.BlockSpec(memory_space=pltpu.VMEM)
SMEM = pl.BlockSpec(memory_space=pltpu.SMEM)
PARAMS = pltpu.CompilerParams(vmem_limit_bytes=48 * 2**20)


def lanes_of(shape):
    return lax.broadcasted_iota(jnp.int32, shape, len(shape) - 1)


def reciprocal(x):
    guess = pl.reciprocal(x, approx=True)
    return guess * (2.0 - x * guess)


def primitive(cons):
    inverse = reciprocal(cons[0])
    vel = [cons[n] * inverse for n in (1, 2, 3)]
    kinetic = 0.5 * (cons[1] * vel[0] + cons[2] * vel[1] + cons[3] * vel[2])
    return [cons[0], *vel, (gamma_ratio - 1.0) * (cons[4] - kinetic)]


def conserved_of(prim):
    mom = [prim[0] * prim[n] for n in (1, 2, 3)]
    kinetic = 0.5 * (mom[0] * prim[1] + mom[1] * prim[2] + mom[2] * prim[3])
    return [prim[0], *mom, prim[4] * (1.0 / (gamma_ratio - 1.0)) + kinetic]


def sound(prim):
    scaled = gamma_ratio * prim[4]
    return scaled * lax.rsqrt(scaled * prim[0])


def flux_of(prim, cons, normal):
    speed = prim[normal]
    flux = [cons[normal]]
    for n in (1, 2, 3):
        term = cons[n] * speed
        flux.append(term + prim[4] if n == normal else term)
    flux.append((cons[4] + prim[4]) * speed)
    return flux


def twice_face(low_flux, low_cons, low_reach, flux, cons, reach):
    top = jnp.maximum(low_reach, reach)
    return [(a + b) - top * (v - u) for a, b, u, v in zip(low_flux, flux, low_cons, cons)]


def minmod(a, b):
    return jnp.maximum(jnp.minimum(a, b), 0.0) + jnp.minimum(jnp.maximum(a, b), 0.0)


def rolled(arrays, by, axis):
    return [pltpu.roll(x, by % x.shape[axis], axis) for x in arrays]


def first_order_faces(prim, cons, speed_of_sound, normal, axis):
    flux = flux_of(prim, cons, normal)
    reach = jnp.abs(prim[normal]) + speed_of_sound
    low_cons = rolled(cons, 1, axis)
    low_flux = [low_cons[normal], *rolled(flux[1:], 1, axis)]
    low_reach = pltpu.roll(reach, 1, axis)
    return twice_face(low_flux, low_cons, low_reach, flux, cons, reach)


def state_at(prim, normal):
    cons = conserved_of(prim)
    return flux_of(prim, cons, normal), cons, jnp.abs(prim[normal]) + sound(prim)


def second_order_faces(prim, normal, axis):
    diff = [x - y for x, y in zip(prim, rolled(prim, 1, axis))]
    half_slope = [0.5 * minmod(a, b) for a, b in zip(diff, rolled(diff, -1, axis))]
    low = rolled([x + s for x, s in zip(prim, half_slope)], 1, axis)
    high = [x - s for x, s in zip(prim, half_slope)]
    return twice_face(*state_at(low, normal), *state_at(high, normal))


def added_sources(cons, prim):
    return {
        1: 2.0 * omega_rate * cons[2],
        2: -(2.0 - shear_rate) * omega_rate * cons[1],
        4: shear_rate * omega_rate * cons[1] * prim[2],
    }


def row_of(ref, *index):
    return [ref[(*index, pl.ds(c * NZ, NZ), slice(None))] for c in range(5)]


def put_row(ref, index, arrays):
    for c in range(5):
        ref[index, pl.ds(c * NZ, NZ), :] = arrays[c]


def prep_kernel(rem_ref, x_ref, xt_ref, lo_ref, hi_ref, edge_ref):
    for c in range(5):
        xt_ref[:, pl.ds(c * NZ, NZ), :] = jnp.swapaxes(x_ref[pl.ds(c * NZ, NZ)], 0, 1)
    lo_ref[...] = xt_ref[:WIDTH]
    hi_ref[...] = xt_ref[NROW - WIDTH :]
    at_low = rem_ref[1] == 0
    first = jnp.where(at_low, 0, NROW - WIDTH)
    by = jnp.where(at_low, (NC - rem_ref[0]) % NC, rem_ref[0])
    for w in range(WIDTH):
        edge_ref[w] = pltpu.roll(xt_ref[first + w], by, 1)


def gather_kernel(rem_ref, xt_ref, up_ref, dn_ref, e1_ref, e2_ref, full_ref, strip_ref):
    rem, rad, last = rem_ref[0], rem_ref[1], rem_ref[2]
    full_ref[pl.ds(WIDTH, NROW)] = xt_ref[...]
    lane = lanes_of((WIDTH, 5 * NZ, NC))

    @pl.when(rad != 0)
    def _():
        full_ref[pl.ds(0, WIDTH)] = up_ref[...]

    @pl.when(rad == 0)
    def _():
        full_ref[pl.ds(0, WIDTH)] = jnp.where(lane >= rem, e1_ref[...], e2_ref[...])

    @pl.when(rad != last)
    def _():
        full_ref[pl.ds(NROW + WIDTH, WIDTH)] = dn_ref[...]

    @pl.when(rad == last)
    def _():
        full_ref[pl.ds(NROW + WIDTH, WIDTH)] = jnp.where(lane < NC - rem, e1_ref[...], e2_ref[...])

    group = lanes_of((5 * NZ, LANES)) // GROUP
    for tile, rows in enumerate((range(WIDTH, WIDTH + NROW), (0, 1, 2, NROW + 3, NROW + 4, NROW + 5))):
        packed = jnp.zeros((5 * NZ, LANES), jnp.float32)
        for g, row in enumerate(rows):
            moved = pltpu.roll(full_ref[row], g * GROUP + GROUP // 2, 1)[:, :LANES]
            packed = jnp.where(group == g, moved, packed)
        strip_ref[:, tile * LANES : (tile + 1) * LANES] = packed


def step_kernel(full_ref, own_ref, left_ref, right_ref, out_ref, prim_ref, half_ref, faces_ref, prev_ref, edge_ref):
    lane = lanes_of((NZ, NC))
    tile_lane = lanes_of((NZ, LANES))
    from_low = (tile_lane % GROUP) < GROUP // 2
    pred = 0.25 * step_ratio
    corr = 0.5 * step_ratio

    def edges(c, tile):
        rows, cols = pl.ds(c * NZ, NZ), pl.ds(tile * LANES, LANES)
        own = own_ref[rows, cols]
        low = jnp.where(from_low, left_ref[rows, cols], own)
        high = jnp.where(from_low, own, right_ref[rows, cols])
        return jnp.concatenate([low, high], axis=1)

    def keep_faces(which, tile, faces):
        for c in range(5):
            for side in range(2):
                faces_ref[which, side, pl.ds(c * NZ, NZ), :] = faces[c][:, side * LANES : (side + 1) * LANES]

    def patched(faces, which, group, count):
        lower, upper = [], []
        for c in range(5):
            rows = pl.ds(c * NZ, NZ)
            left = pltpu.roll(faces_ref[which, 0, rows, :], (2 * LANES - GROUP * group - GROUP // 2) % LANES, 1)
            tiles = [jnp.where(tile_lane < count, left, faces[c][:, :LANES]), faces[c][:, LANES:]]
            right = faces_ref[which, 1, rows, :]
            beyond = pltpu.roll(right, (2 * LANES - 1 - GROUP * group - GROUP // 2) % LANES, 1)
            if count > 1:
                inside = pltpu.roll(right, (2 * LANES - GROUP * group - GROUP // 2) % LANES, 1)
                tiles[1] = jnp.where(tile_lane == LANES - 1, inside, tiles[1])
            whole = jnp.concatenate(tiles, axis=1)
            lower.append(whole)
            above = pltpu.roll(whole, NC - 1, 1)
            upper.append(
                jnp.concatenate(
                    [above[:, :LANES], jnp.where(tile_lane == LANES - 1, beyond, above[:, LANES:])], axis=1
                )
            )
        return lower, upper

    ghost = [edges(c, 1) for c in range(5)]
    ghost_prim = primitive(ghost)
    keep_faces(1, 1, first_order_faces(ghost_prim, ghost, sound(ghost_prim), 2, 1))
    cons = [edges(c, 0) for c in range(5)]
    prim = primitive(cons)
    speed = sound(prim)
    az = first_order_faces(prim, cons, speed, 2, 1)
    keep_faces(0, 0, az)
    vert = first_order_faces(prim, cons, speed, 3, 0)
    in_tile = lane % LANES
    below = [
        jnp.where(in_tile < GROUP, a, b) for a, b in zip(rolled(ghost, -2 * GROUP, 1), rolled(cons, GROUP, 1))
    ]
    above = [
        jnp.where(in_tile >= LANES - GROUP, a, b)
        for a, b in zip(rolled(ghost, LANES - 4 * GROUP, 1), rolled(cons, -GROUP, 1))
    ]

    def rad_state(u):
        q = primitive(u)
        return flux_of(q, u, 1), u, jnp.abs(q[1]) + sound(q)

    mid_state = (flux_of(prim, cons, 1), cons, jnp.abs(prim[1]) + speed)
    rad_low = twice_face(*rad_state(below), *mid_state)
    rad_high = twice_face(*mid_state, *rad_state(above))
    source = added_sources(cons, prim)
    half = []
    for c in range(5):
        total = (rad_high[c] - rad_low[c]) + (pltpu.roll(az[c], NC - 1, 1) - az[c])
        total = total + (pltpu.roll(vert[c], NZ - 1, 0) - vert[c])
        value = cons[c] - pred * total
        half.append(value + 0.5 * step_ratio * source[c] if c in source else value)
    az = second_order_faces(primitive(half), 2, 1)
    for c in range(5):
        for side in range(2):
            edge_ref[side, pl.ds(c * NZ, NZ), :] = az[c][:, side * LANES : (side + 1) * LANES]

    def predict(i, carry):
        cons = row_of(full_ref, i)
        prim = primitive(cons)
        speed = sound(prim)
        flux = flux_of(prim, cons, 1)
        reach = jnp.abs(prim[1]) + speed

        @pl.when(i > 0)
        def _():
            low_cons = row_of(full_ref, i - 1)
            low_flux = row_of(prev_ref, 0)
            low_reach = prev_ref[1, pl.ds(0, NZ), :]
            rad = twice_face(low_flux, low_cons, low_reach, flux, cons, reach)

            @pl.when(i > 1)
            def _():
                done = [x - pred * y for x, y in zip(row_of(half_ref, 0), rad)]
                put_row(prim_ref, i - 1, primitive(done))

            @pl.when(i < NFULL - 1)
            def _():
                interior = jnp.logical_and(i >= WIDTH, i < WIDTH + NROW)
                which = jnp.where(interior, 0, 1)
                group = jnp.where(interior, i - WIDTH, jnp.where(i < WIDTH, i, i - NROW))
                lower, upper = patched(first_order_faces(prim, cons, speed, 2, 1), which, group, 1)
                vert = first_order_faces(prim, cons, speed, 3, 0)
                source = added_sources(cons, prim)
                for c in range(5):
                    total = (upper[c] - lower[c]) + (pltpu.roll(vert[c], NZ - 1, 0) - vert[c]) - rad[c]
                    value = cons[c] - pred * total
                    if c in source:
                        value = value + 0.5 * step_ratio * source[c]
                    half_ref[0, pl.ds(c * NZ, NZ), :] = value

        put_row(prev_ref, 0, flux)
        prev_ref[1, pl.ds(0, NZ), :] = reach
        return carry

    lax.fori_loop(0, NFULL, predict, 0)

    faces_ref[0] = edge_ref[...]

    def correct(i, carry):
        prim = row_of(prim_ref, i)
        half_slope = [
            0.5 * minmod(x - a, b - x) for x, a, b in zip(prim, row_of(prim_ref, i - 1), row_of(prim_ref, i + 1))
        ]
        high = [x - s for x, s in zip(prim, half_slope)]

        @pl.when(i > WIDTH - 1)
        def _():
            rad = twice_face(*state_at(row_of(prev_ref, 0), 1), *state_at(high, 1))

            @pl.when(i > WIDTH)
            def _():
                for c in range(5):
                    out_ref[i - WIDTH - 1, pl.ds(c * NZ, NZ), :] = half_ref[0, pl.ds(c * NZ, NZ), :] - corr * rad[c]

            @pl.when(i < WIDTH + NROW)
            def _():
                lower, upper = patched(second_order_faces(prim, 2, 1), 0, i - WIDTH, 2)
                vert = second_order_faces(prim, 3, 0)
                source = added_sources(conserved_of(prim), prim)
                for c in range(5):
                    total = (upper[c] - lower[c]) + (pltpu.roll(vert[c], NZ - 1, 0) - vert[c]) - rad[c]
                    value = full_ref[i, pl.ds(c * NZ, NZ), :] - corr * total
                    if c in source:
                        value = value + step_ratio * source[c]
                    half_ref[0, pl.ds(c * NZ, NZ), :] = value

        put_row(prev_ref, 0, [x + s for x, s in zip(prim, half_slope)])
        return carry

    lax.fori_loop(WIDTH - 1, WIDTH + NROW + 1, correct, 0)


def remap_kernel(count, shift_ref, frac_ref, x_ref, o_ref, held_ref):
    row = shift_ref[NROW]
    shift, frac = shift_ref[row], frac_ref[row]
    hop = jnp.bitwise_and(jnp.right_shift(shift, 8), count - 1)
    rem = jnp.bitwise_and(shift, NC - 1)
    lane = lanes_of((5 * NZ, NC))

    def one(m, carry):
        here = jnp.bitwise_and(m + count - 1, count - 1)
        before = jnp.bitwise_and(m + count - 2, count - 1)
        block = x_ref[here]
        lower = jnp.where(lane == 0, pltpu.roll(x_ref[before], 1, 1), pltpu.roll(block, 1, 1))
        moved = pltpu.roll((1.0 - frac) * block + frac * lower, rem, 1)

        @pl.when(m > 0)
        def _():
            o_ref[jnp.bitwise_and(m + hop + count - 1, count - 1)] = jnp.where(lane >= rem, moved, held_ref[...])

        held_ref[...] = moved
        return carry

    lax.fori_loop(0, count + 1, one, 0)


def finish_kernel(y_ref, o_ref):
    for c in range(5):
        o_ref[pl.ds(c * NZ, NZ)] = jnp.swapaxes(y_ref[:, pl.ds(c * NZ, NZ), :], 0, 1)


def shape(*dims):
    return jax.ShapeDtypeStruct(dims, jnp.float32)


def local(conserved, shift_cells, shift_frac, boundary_offset):
    azs, rads = lax.axis_size("az"), lax.axis_size("rad")
    az, rad = lax.axis_index("az"), lax.axis_index("rad")
    offset = boundary_offset[0]
    hop, rem = offset // NC, offset % NC
    scalars = jnp.stack([rem, rad, jnp.int32(rads - 1)]).astype(jnp.int32)
    rim = shape(WIDTH, 5 * NZ, NC)
    rows, lo, hi, edge = pl.pallas_call(
        prep_kernel,
        out_shape=(shape(NROW, 5 * NZ, NC), rim, rim, rim),
        in_specs=[SMEM, VMEM],
        out_specs=(VMEM,) * 4,
        compiler_params=PARAMS,
    )(scalars, conserved.reshape(5 * NZ, NROW, NC))

    from_below = lax.ppermute(hi, "rad", [(i, i + 1) for i in range(rads - 1)])
    from_above = lax.ppermute(lo, "rad", [(i + 1, i) for i in range(rads - 1)])

    def ends(k):
        pairs = [(a * rads + rads - 1, (a + k) % azs * rads) for a in range(azs)]
        return pairs + [(b, a) for a, b in pairs]

    def moved_by(k):
        def send(block):
            return tuple(lax.ppermute(block, ("az", "rad"), ends(j % azs)) for j in (k, k + 1))

        return send

    first, second = lax.switch(hop, [moved_by(k) for k in range(azs)], edge)
    full, strip = pl.pallas_call(
        gather_kernel,
        out_shape=(shape(NFULL, 5 * NZ, NC), shape(5 * NZ, 2 * LANES)),
        in_specs=[SMEM] + [VMEM] * 5,
        out_specs=(VMEM,) * 2,
        compiler_params=PARAMS,
    )(scalars, rows, from_below, from_above, first, second)
    left = lax.ppermute(strip, "az", [(i, (i + 1) % azs) for i in range(azs)])
    right = lax.ppermute(strip, "az", [((i + 1) % azs, i) for i in range(azs)])
    updated = pl.pallas_call(
        step_kernel,
        out_shape=shape(NROW, 5 * NZ, NC),
        in_specs=[VMEM] * 4,
        out_specs=VMEM,
        scratch_shapes=[
            pltpu.VMEM((NFULL, 5 * NZ, NC), jnp.float32),
            pltpu.VMEM((1, 5 * NZ, NC), jnp.float32),
            pltpu.VMEM((2, 2, 5 * NZ, LANES), jnp.float32),
            pltpu.VMEM((2, 5 * NZ, NC), jnp.float32),
            pltpu.VMEM((2, 5 * NZ, LANES), jnp.float32),
        ],
        compiler_params=PARAMS,
    )(full, strip, left, right)

    whole_row = lax.all_to_all(updated, "az", 0, 0, tiled=True)
    shifts = jnp.concatenate([shift_cells, az[None].astype(jnp.int32)])
    moved = pl.pallas_call(
        functools.partial(remap_kernel, azs),
        out_shape=shape(azs, 5 * NZ, NC),
        in_specs=[SMEM, SMEM, VMEM],
        out_specs=VMEM,
        scratch_shapes=[pltpu.VMEM((5 * NZ, NC), jnp.float32)],
        compiler_params=PARAMS,
    )(shifts, shift_frac, whole_row)
    back = lax.all_to_all(moved, "az", 0, 0, tiled=True)
    result = pl.pallas_call(
        finish_kernel,
        out_shape=shape(5 * NZ, NROW, NC),
        in_specs=[VMEM],
        out_specs=VMEM,
        compiler_params=PARAMS,
    )(back)
    return result.reshape(5, NZ, NROW, NC)


def solution(mesh):
    in_specs = (P(None, None, "rad", "az"), P("rad"), P("rad"), P())
    out_specs = P(None, None, "rad", "az")
    return jax.shard_map(local, mesh=mesh, in_specs=in_specs, out_specs=out_specs, check_vma=False)
```

profile of v0, /device:TPU:1, one launch (start us, length us, event | category | flops | bytes accessed | tf_op | source)
XLA Modules:
  0.0 111.2 jit_solution(16891382651858611481)
XLA Ops:
  0.7 0.1 pad_add_fusion.1.rem_ref
  0.8 0.0 copy-start
  0.8 1.3 %copy-done = f32[5,16,16,256]{3,2,1,0:T(8,128)S(1)} copy-done((f32[5,16,16,256]{3,2,1,0:T(8,128)S(1)}, f32[5,16,16,256]{3,2,1,0:T(8,128)}, u32[]{:S(2)}) %copy-start) | copy-done | bytes 1310744
  2.1 0.9 shard_map.46
  3.0 4.1 %collective-permute-start.32 = (f32[3,80,256]{2,1,0:T(8,128)S(1)}, f32[3,80,256]{2,1,0:T(8,128)S(1)}, u32[]{:S(2)}, u32[]{:S(2)}) collective-permute-start(f32[3,80,256]{2,1,0:T(8,128)S(1)} %get-tuple-element.30), channel_id=1, source_target_pairs={{0,1},{1,2},{2,3},{3,4},{4,5},{5,6},{6,7},{8,9},{9,10},{10,11},{11... | collective-permute-start | bytes 737288 | tf_op jit(solution)/shard_map/ppermute | solution.py:359
  7.1 1.3 %collective-permute-start.33 = (f32[3,80,256]{2,1,0:T(8,128)S(1)}, f32[3,80,256]{2,1,0:T(8,128)S(1)}, u32[]{:S(2)}, u32[]{:S(2)}) collective-permute-start(f32[3,80,256]{2,1,0:T(8,128)S(1)} %get-tuple-element.31), channel_id=1, source_target_pairs={{1,0},{2,1},{3,2},{4,3},{5,4},{6,5},{7,6},{9,8},{10,9},{11,10},{12... | collective-permute-start | bytes 737288 | tf_op jit(solution)/shard_map/ppermute | solution.py:360
  8.4 20.9 %conditional.1 = (f32[3,80,256]{2,1,0:T(8,128)}, f32[3,80,256]{2,1,0:T(8,128)}) conditional(s32[]{:T(128)} %clamp.3, f32[3,80,256]{2,1,0:T(8,128)S(1)} %get-tuple-element.32, f32[3,80,256]{2,1,0:T(8,128)S(1)} %get-tuple-element.32, f32[3,80,256]{2,1,0:T(8,128)S(1)} %get-tuple-element.32, ...), branch_computations={%region_0.1_spmd, %region_1.2_spmd, %region_2.3_spmd, %region_3.4_... | conditional | bytes 1966176 | solution.py:372
  8.4 9.0 %collective-permute-start.19 = (f32[3,80,256]{2,1,0:T(8,128)S(1)}, f32[3,80,256]{2,1,0:T(8,128)}, u32[]{:S(2)}, u32[]{:S(2)}) collective-permute-start(f32[3,80,256]{2,1,0:T(8,128)S(1)} %param.9), channel_id=1, source_target_pairs={{7,80},{15,88},{23,96},{31,104},{39,112},{47,120},{55,0},{63,8},{7... | collective-permute-start | bytes 737288 | tf_op jit(solution)/shard_map/cond/branch_9_fun/ppermute | solution.py:368
  17.4 3.0 %collective-permute-start.18 = (f32[3,80,256]{2,1,0:T(8,128)S(1)}, f32[3,80,256]{2,1,0:T(8,128)}, u32[]{:S(2)}, u32[]{:S(2)}) collective-permute-start(f32[3,80,256]{2,1,0:T(8,128)S(1)} %param.9), channel_id=1, source_target_pairs={{7,72},{15,80},{23,88},{31,96},{39,104},{47,112},{55,120},{63,0},{... | collective-permute-start | bytes 737288 | tf_op jit(solution)/shard_map/cond/branch_9_fun/ppermute | solution.py:368
  20.4 2.2 %collective-permute-done.19 = f32[3,80,256]{2,1,0:T(8,128)} collective-permute-done((f32[3,80,256]{2,1,0:T(8,128)S(1)}, f32[3,80,256]{2,1,0:T(8,128)}, u32[]{:S(2)}, u32[]{:S(2)}) %collective-permute-start.19) | collective-permute-done | bytes 245792 | tf_op jit(solution)/shard_map/cond/branch_9_fun/ppermute | solution.py:368
  22.6 6.7 %collective-permute-done.18 = f32[3,80,256]{2,1,0:T(8,128)} collective-permute-done((f32[3,80,256]{2,1,0:T(8,128)S(1)}, f32[3,80,256]{2,1,0:T(8,128)}, u32[]{:S(2)}, u32[]{:S(2)}) %collective-permute-start.18) | collective-permute-done | bytes 245792 | tf_op jit(solution)/shard_map/cond/branch_9_fun/ppermute | solution.py:368
  29.3 0.0 collective-permute-done.32.up_ref
  29.3 0.0 collective-permute-done.33.dn_ref
  29.3 1.7 %shard_map.47 = (f32[22,80,256]{2,1,0:T(8,128)S(1)}, f32[80,256]{1,0:T(8,128)S(1)}) custom-call(s32[3]{0:T(128)S(1)} %pad_add_fusion.1.rem_ref, f32[16,80,256]{2,1,0:T(8,128)S(1)} %get-tuple-element.29.xt_ref, f32[3,80,256]{2,1,0:T(8,128)S(1)} %collective-permute-done.32.up_ref, f32[3,80,256]{2,1,0:T(8,128)S(1)} %collective-permute-done.33.dn_ref, ...), custom_call_target="tpu_custom_call" | custom-call | tf_op jit(solution)/shard_map/pallas_call | solution.py:373
  31.0 2.6 %collective-permute-start.35 = (f32[80,256]{1,0:T(8,128)S(1)}, f32[80,256]{1,0:T(8,128)S(1)}, u32[]{:S(2)}, u32[]{:S(2)}) collective-permute-start(f32[80,256]{1,0:T(8,128)S(1)} %get-tuple-element.36.own_ref), channel_id=1, source_target_pairs={{8,0},{16,8},{24,16},{32,24},{40,32},{48,40},{56,48},{64,56},{72,6... | collective-permute-start | bytes 245768 | tf_op jit(solution)/shard_map/ppermute | solution.py:381
  33.6 0.2 collective-permute-start.34
  33.8 2.0 %collective-permute-done.35.right_ref = f32[80,256]{1,0:T(8,128)S(1)} collective-permute-done((f32[80,256]{1,0:T(8,128)S(1)}, f32[80,256]{1,0:T(8,128)S(1)}, u32[]{:S(2)}, u32[]{:S(2)}) %collective-permute-start.35) | collective-permute-done | bytes 81952 | tf_op jit(solution)/shard_map/ppermute | solution.py:381
  35.8 0.4 collective-permute-done.34.left_ref
  36.3 14.9 %shard_map.48 = f32[16,80,256]{2,1,0:T(8,128)} custom-call(f32[22,80,256]{2,1,0:T(8,128)S(1)} %get-tuple-element.35.full_ref, f32[80,256]{1,0:T(8,128)S(1)} %get-tuple-element.36.own_ref, f32[80,256]{1,0:T(8,128)S(1)} %collective-permute-done.34.left_ref, f32[80,256]{1,0:T(8,128)S(1)} %collective-permute-done.35.right_ref), custom_call_target="tpu_custom_call" | custom-call | tf_op jit(solution)/shard_map/pallas_call | solution.py:382
  51.2 0.0 copy-start.2
  51.2 0.0 copy-start.1
  51.2 11.5 %all-to-all-start = ((f32[16,80,256]{2,1,0:T(8,128)}), f32[16,80,256]{2,1,0:T(8,128)S(1)}, u32[]{:S(2)}, u32[]{:S(2)}) async-start(f32[16,80,256]{2,1,0:T(8,128)} %shard_map.48), calls=%async_computation | async-start | bytes 2621440 | tf_op jit(solution)/shard_map/all_to_all | solution.py:397
  62.7 0.0 copy-done.2
  62.7 0.1 pad_add_fusion.shift_ref
  62.8 20.1 %all-to-all-done.x_ref = f32[16,80,256]{2,1,0:T(8,128)S(1)} async-done(((f32[16,80,256]{2,1,0:T(8,128)}), f32[16,80,256]{2,1,0:T(8,128)S(1)}, u32[]{:S(2)}, u32[]{:S(2)}) %all-to-all-start) | async-done | bytes 1310752 | tf_op jit(solution)/shard_map/all_to_all | solution.py:397
  82.9 0.0 copy-done.1
  82.9 3.9 %shard_map.49 = f32[16,80,256]{2,1,0:T(8,128)S(1)} custom-call(s32[17]{0:T(128)S(1)} %pad_add_fusion.shift_ref, f32[16]{0:T(128)S(1)} %copy-done.1, f32[16,80,256]{2,1,0:T(8,128)S(1)} %all-to-all-done.x_ref), custom_call_target="tpu_custom_call" | custom-call | tf_op jit(solution)/shard_map/pallas_call | solution.py:399
  86.8 23.1 %all_to_all.10.y_ref = f32[16,80,256]{2,1,0:T(8,128)S(1)} all-to-all(f32[16,80,256]{2,1,0:T(8,128)S(1)} %shard_map.49), channel_id=1, replica_groups=mesh['az'=16,'rad'=8] {'az'}, dimensions={0} | all-to-all | bytes 2621440 | tf_op jit(solution)/shard_map/all_to_all | solution.py:407
  109.9 1.3 %shard_map.50 = f32[80,16,256]{2,1,0:T(8,128)} custom-call(f32[16,80,256]{2,1,0:T(8,128)S(1)} %all_to_all.10.y_ref), custom_call_target="tpu_custom_call" | custom-call | tf_op jit(solution)/shard_map/pallas_call | solution.py:408
Async XLA Ops:
  0.8 1.3 %copy-start = (f32[5,16,16,256]{3,2,1,0:T(8,128)S(1)}, f32[5,16,16,256]{3,2,1,0:T(8,128)}, u32[]{:S(2)}) copy-start(f32[5,16,16,256]{3,2,1,0:T(8,128)} %param.20) | copy-start | bytes 3932164
  3.0 26.3 %collective-permute-start.32 = (f32[3,80,256]{2,1,0:T(8,128)S(1)}, f32[3,80,256]{2,1,0:T(8,128)S(1)}, u32[]{:S(2)}, u32[]{:S(2)}) collective-permute-start(f32[3,80,256]{2,1,0:T(8,128)S(1)} %get-tuple-element.30), channel_id=1, source_target_pairs={{0,1},{1,2},{2,3},{3,4},{4,5},{5,6},{6,7},{8,9},{9,10},{10,11},{11... | collective-permute-start | bytes 737288 | tf_op jit(solution)/shard_map/ppermute | solution.py:359
  7.1 22.2 %collective-permute-start.33 = (f32[3,80,256]{2,1,0:T(8,128)S(1)}, f32[3,80,256]{2,1,0:T(8,128)S(1)}, u32[]{:S(2)}, u32[]{:S(2)}) collective-permute-start(f32[3,80,256]{2,1,0:T(8,128)S(1)} %get-tuple-element.31), channel_id=1, source_target_pairs={{1,0},{2,1},{3,2},{4,3},{5,4},{6,5},{7,6},{9,8},{10,9},{11,10},{12... | collective-permute-start | bytes 737288 | tf_op jit(solution)/shard_map/ppermute | solution.py:360
  8.4 14.1 %collective-permute-start.19 = (f32[3,80,256]{2,1,0:T(8,128)S(1)}, f32[3,80,256]{2,1,0:T(8,128)}, u32[]{:S(2)}, u32[]{:S(2)}) collective-permute-start(f32[3,80,256]{2,1,0:T(8,128)S(1)} %param.9), channel_id=1, source_target_pairs={{7,80},{15,88},{23,96},{31,104},{39,112},{47,120},{55,0},{63,8},{7... | collective-permute-start | bytes 737288 | tf_op jit(solution)/shard_map/cond/branch_9_fun/ppermute | solution.py:368
  17.4 11.8 %collective-permute-start.18 = (f32[3,80,256]{2,1,0:T(8,128)S(1)}, f32[3,80,256]{2,1,0:T(8,128)}, u32[]{:S(2)}, u32[]{:S(2)}) collective-permute-start(f32[3,80,256]{2,1,0:T(8,128)S(1)} %param.9), channel_id=1, source_target_pairs={{7,72},{15,80},{23,88},{31,96},{39,104},{47,112},{55,120},{63,0},{... | collective-permute-start | bytes 737288 | tf_op jit(solution)/shard_map/cond/branch_9_fun/ppermute | solution.py:368
  31.0 4.8 %collective-permute-start.35 = (f32[80,256]{1,0:T(8,128)S(1)}, f32[80,256]{1,0:T(8,128)S(1)}, u32[]{:S(2)}, u32[]{:S(2)}) collective-permute-start(f32[80,256]{1,0:T(8,128)S(1)} %get-tuple-element.36.own_ref), channel_id=1, source_target_pairs={{8,0},{16,8},{24,16},{32,24},{40,32},{48,40},{56,48},{64,56},{72,6... | collective-permute-start | bytes 245768 | tf_op jit(solution)/shard_map/ppermute | solution.py:381
  33.6 2.7 %collective-permute-start.34 = (f32[80,256]{1,0:T(8,128)S(1)}, f32[80,256]{1,0:T(8,128)S(1)}, u32[]{:S(2)}, u32[]{:S(2)}) collective-permute-start(f32[80,256]{1,0:T(8,128)S(1)} %get-tuple-element.36.own_ref), channel_id=1, source_target_pairs={{0,8},{8,16},{16,24},{24,32},{32,40},{40,48},{48,56},{56,64},{64,7... | collective-permute-start | bytes 245768 | tf_op jit(solution)/shard_map/ppermute | solution.py:380
  51.2 11.5 %copy-start.2 = (s32[16]{0:T(128)S(1)}, s32[16]{0:T(128)}, u32[]{:S(2)}) copy-start(s32[16]{0:T(128)} %param.21) | copy-start | bytes 196
  51.2 31.7 %copy-start.1 = (f32[16]{0:T(128)S(1)}, f32[16]{0:T(128)}, u32[]{:S(2)}) copy-start(f32[16]{0:T(128)} %frac_ref.1) | copy-start | bytes 196
  51.2 31.7 %all-to-all-start = ((f32[16,80,256]{2,1,0:T(8,128)}), f32[16,80,256]{2,1,0:T(8,128)S(1)}, u32[]{:S(2)}, u32[]{:S(2)}) async-start(f32[16,80,256]{2,1,0:T(8,128)} %shard_map.48), calls=%async_computation | async-start | bytes 2621440 | tf_op jit(solution)/shard_map/all_to_all | solution.py:397
where the time goes:
time: 112 us; the launch traced here: 111 us
  starting transfers between devices  31.6 us (28%)
  waiting for transfers between devices  31.4 us (28%)
  blocking collectives  23.1 us (21%)
  Pallas kernels  22.8 us (20%)
  local copies, waits for them, and re-layouts  1.33 us (1%)
    all_to_all x1, blocking collectives, local(): back = lax.all_to_all(moved, 'az', 0, 0, tiled=True)  23.1 us
    all_to_all x1, waiting for transfers between devices, local(): whole_row = lax.all_to_all(updated, 'az', 0, 0, tiled=True)  20.1 us
    pallas_call x1, Pallas kernels, local(): pl.pallas_call(step_kernel, out_shape=shape(NROW, 5 * NZ, NC), in_specs=[...  14.9 us
    ppermute x2, starting transfers between devices, send(): lax.ppermute(block, ('az', 'rad'), ends(j % azs))  11.9 us
    all_to_all x1, starting transfers between devices, local(): whole_row = lax.all_to_all(updated, 'az', 0, 0, tiled=True)  11.5 us
    ppermute x2, waiting for transfers between devices, send(): lax.ppermute(block, ('az', 'rad'), ends(j % azs))  8.87 us
    ppermute x1, starting transfers between devices, local(): from_below = lax.ppermute(hi, 'rad', [(i, i + 1) for i in range(rads - 1)])  4.09 us
    pallas_call x1, Pallas kernels, local(): pl.pallas_call(functools.partial(remap_kernel, azs), out_shape=shape(azs,...  3.9 us
  transfers between devices with their start and end apart: 7, of which 5 were waited for; matrix products, arithmetic and copies ran while one was open for 0% of the time, Pallas kernels for 0%

commit v1 on v0

v1 whole, which is shorter than its diff:
```python
import functools

import jax
import jax.numpy as jnp
from jax import lax
from jax.experimental import pallas as pl
from jax.experimental.pallas import tpu as pltpu
from jax.sharding import PartitionSpec as P

gamma_ratio = 5.0 / 3.0
step_ratio = 0.06
omega_rate = 1.0
shear_rate = 1.5

NZ = 16
NROW = 16
NC = 256
LANES = 128
WIDTH = 3
PRED = 0.25 * step_ratio
CORR = 0.5 * step_ratio
GROUP = 8
VMEM = pl.BlockSpec(memory_space=pltpu.VMEM)
SMEM = pl.BlockSpec(memory_space=pltpu.SMEM)
PARAMS = pltpu.CompilerParams(vmem_limit_bytes=48 * 2**20)


def lanes_of(shape):
    return lax.broadcasted_iota(jnp.int32, shape, len(shape) - 1)


def reciprocal(x):
    guess = pl.reciprocal(x, approx=True)
    return guess * (2.0 - x * guess)


def primitive(cons):
    inverse = reciprocal(cons[0])
    vel = [cons[n] * inverse for n in (1, 2, 3)]
    kinetic = 0.5 * (cons[1] * vel[0] + cons[2] * vel[1] + cons[3] * vel[2])
    return [cons[0], *vel, (gamma_ratio - 1.0) * (cons[4] - kinetic)]


def conserved_of(prim):
    mom = [prim[0] * prim[n] for n in (1, 2, 3)]
    kinetic = 0.5 * (mom[0] * prim[1] + mom[1] * prim[2] + mom[2] * prim[3])
    return [prim[0], *mom, prim[4] * (1.0 / (gamma_ratio - 1.0)) + kinetic]


def sound(prim):
    scaled = gamma_ratio * prim[4]
    return scaled * lax.rsqrt(scaled * prim[0])


def flux_of(prim, cons, normal):
    speed = prim[normal]
    flux = [cons[normal]]
    for n in (1, 2, 3):
        term = cons[n] * speed
        flux.append(term + prim[4] if n == normal else term)
    flux.append((cons[4] + prim[4]) * speed)
    return flux


def twice_face(low_flux, low_cons, low_reach, flux, cons, reach):
    top = jnp.maximum(low_reach, reach)
    return [(a + b) - top * (v - u) for a, b, u, v in zip(low_flux, flux, low_cons, cons)]


def minmod(a, b):
    return jnp.maximum(jnp.minimum(a, b), 0.0) + jnp.minimum(jnp.maximum(a, b), 0.0)


def rolled(arrays, by, axis):
    return [pltpu.roll(x, by % x.shape[axis], axis) for x in arrays]


def first_order_faces(prim, cons, speed_of_sound, normal, axis):
    flux = flux_of(prim, cons, normal)
    reach = jnp.abs(prim[normal]) + speed_of_sound
    low_cons = rolled(cons, 1, axis)
    low_flux = [low_cons[normal], *rolled(flux[1:], 1, axis)]
    low_reach = pltpu.roll(reach, 1, axis)
    return twice_face(low_flux, low_cons, low_reach, flux, cons, reach)


def state_at(prim, normal):
    cons = conserved_of(prim)
    return flux_of(prim, cons, normal), cons, jnp.abs(prim[normal]) + sound(prim)


def second_order_faces(prim, normal, axis):
    diff = [x - y for x, y in zip(prim, rolled(prim, 1, axis))]
    half_slope = [0.5 * minmod(a, b) for a, b in zip(diff, rolled(diff, -1, axis))]
    low = rolled([x + s for x, s in zip(prim, half_slope)], 1, axis)
    high = [x - s for x, s in zip(prim, half_slope)]
    return twice_face(*state_at(low, normal), *state_at(high, normal))


def added_sources(cons, prim):
    return {
        1: 2.0 * omega_rate * cons[2],
        2: -(2.0 - shear_rate) * omega_rate * cons[1],
        4: shear_rate * omega_rate * cons[1] * prim[2],
    }


def row_of(ref, *index):
    return [ref[(*index, pl.ds(c * NZ, NZ), slice(None))] for c in range(5)]


def put_row(ref, index, arrays):
    for c in range(5):
        ref[index, pl.ds(c * NZ, NZ), :] = arrays[c]


def tile_lanes():
    return lanes_of((NZ, LANES))


def edge_faces_of(strip):
    prim = primitive(strip)
    speed = sound(prim)
    return prim, speed, first_order_faces(prim, strip, speed, 2, 1)


def keep_faces(ref, faces):
    for c in range(5):
        for side in range(2):
            ref[side, pl.ds(c * NZ, NZ), :] = faces[c][:, side * LANES : (side + 1) * LANES]


def strip_half(cons, prim, speed, az, below, above):
    def rad_state(u):
        q = primitive(u)
        return flux_of(q, u, 1), u, jnp.abs(q[1]) + sound(q)

    mid_state = (flux_of(prim, cons, 1), cons, jnp.abs(prim[1]) + speed)
    rad_low = twice_face(*rad_state(below), *mid_state)
    rad_high = twice_face(*mid_state, *rad_state(above))
    vert = first_order_faces(prim, cons, speed, 3, 0)
    source = added_sources(cons, prim)
    half = []
    for c in range(5):
        total = (rad_high[c] - rad_low[c]) + (pltpu.roll(az[c], NC - 1, 1) - az[c])
        total = total + (pltpu.roll(vert[c], NZ - 1, 0) - vert[c])
        value = cons[c] - PRED * total
        half.append(value + 0.5 * step_ratio * source[c] if c in source else value)
    return half


def patched(faces, faces_ref, group, count):
    lane = tile_lanes()
    lower, upper = [], []
    for c in range(5):
        rows = pl.ds(c * NZ, NZ)
        at_edge = (2 * LANES - GROUP * group - GROUP // 2) % LANES
        before_edge = (3 * LANES - 1 - GROUP * group - GROUP // 2) % LANES
        left = pltpu.roll(faces_ref[0, rows, :], at_edge, 1)
        tiles = [jnp.where(lane < count, left, faces[c][:, :LANES]), faces[c][:, LANES:]]
        right = faces_ref[1, rows, :]
        beyond = pltpu.roll(right, before_edge, 1)
        if count > 1:
            tiles[1] = jnp.where(lane == LANES - 1, pltpu.roll(right, at_edge, 1), tiles[1])
        whole = jnp.concatenate(tiles, axis=1)
        lower.append(whole)
        above = pltpu.roll(whole, NC - 1, 1)
        last = jnp.where(lane == LANES - 1, beyond, above[:, LANES:])
        upper.append(jnp.concatenate([above[:, :LANES], last], axis=1))
    return lower, upper


def predict(count, load, faces_at, sink, half_ref, prev_ref):
    def step(i, carry):
        cons = load(i)
        prim = primitive(cons)
        speed = sound(prim)
        flux = flux_of(prim, cons, 1)
        reach = jnp.abs(prim[1]) + speed

        @pl.when(i > 0)
        def _():
            low_reach = prev_ref[1, pl.ds(0, NZ), :]
            rad = twice_face(row_of(prev_ref, 0), load(i - 1), low_reach, flux, cons, reach)

            @pl.when(i > 1)
            def _():
                sink(i - 1, primitive([x - PRED * y for x, y in zip(row_of(half_ref, 0), rad)]))

            @pl.when(i < count - 1)
            def _():
                lower, upper = patched(first_order_faces(prim, cons, speed, 2, 1), *faces_at(i), 1)
                vert = first_order_faces(prim, cons, speed, 3, 0)
                source = added_sources(cons, prim)
                for c in range(5):
                    total = (upper[c] - lower[c]) + (pltpu.roll(vert[c], NZ - 1, 0) - vert[c]) - rad[c]
                    value = cons[c] - PRED * total
                    if c in source:
                        value = value + 0.5 * step_ratio * source[c]
                    half_ref[0, pl.ds(c * NZ, NZ), :] = value

        put_row(prev_ref, 0, flux)
        prev_ref[1, pl.ds(0, NZ), :] = reach
        return carry

    lax.fori_loop(0, count, step, 0)


def correct(count, load, cons_at, faces_ref, group_of, sink, half_ref, prev_ref):
    def step(i, carry):
        prim = load(i)
        half_slope = [0.5 * minmod(x - a, b - x) for x, a, b in zip(prim, load(i - 1), load(i + 1))]
        high = [x - s for x, s in zip(prim, half_slope)]

        @pl.when(i > 0)
        def _():
            rad = twice_face(*state_at(row_of(prev_ref, 0), 1), *state_at(high, 1))

            @pl.when(i > 1)
            def _():
                sink(i - 1, [x - CORR * y for x, y in zip(row_of(half_ref, 0), rad)])

            @pl.when(i < count - 1)
            def _():
                lower, upper = patched(second_order_faces(prim, 2, 1), faces_ref, group_of(i), 2)
                vert = second_order_faces(prim, 3, 0)
                source = added_sources(conserved_of(prim), prim)
                cons = cons_at(i)
                for c in range(5):
                    total = (upper[c] - lower[c]) + (pltpu.roll(vert[c], NZ - 1, 0) - vert[c]) - rad[c]
                    value = cons[c] - CORR * total
                    if c in source:
                        value = value + step_ratio * source[c]
                    half_ref[0, pl.ds(c * NZ, NZ), :] = value

        put_row(prev_ref, 0, [x + s for x, s in zip(prim, half_slope)])
        return carry

    lax.fori_loop(0, count, step, 0)


def prep_kernel(x_ref, xt_ref, own_ref):
    for c in range(5):
        xt_ref[:, pl.ds(c * NZ, NZ), :] = jnp.swapaxes(x_ref[pl.ds(c * NZ, NZ)], 0, 1)
    group = lanes_of((5 * NZ, LANES)) // GROUP
    packed = jnp.zeros((5 * NZ, LANES), jnp.float32)
    for row in range(NROW):
        moved = pltpu.roll(xt_ref[row], row * GROUP + GROUP // 2, 1)[:, :LANES]
        packed = jnp.where(group == row, moved, packed)
    own_ref[...] = packed


def rims_kernel(rem_ref, xt_ref, own_ref, left_ref, right_ref, strip_ref, up_ref, dn_ref, end_ref):
    lane = lanes_of((5 * NZ, LANES))
    from_low = (lane % GROUP) < GROUP // 2
    own = own_ref[...]
    low = jnp.where(from_low, left_ref[...], own)
    high = jnp.where(from_low, own, right_ref[...])
    strip_ref[:, :LANES] = low
    strip_ref[:, LANES:] = high
    for ref, first in ((dn_ref, 0), (up_ref, NROW - WIDTH)):
        for w in range(WIDTH):
            for side in range(2):
                ref[2 * w + side] = xt_ref[first + w, :, side * LANES : (side + 1) * LANES]
        three = WIDTH * GROUP
        by = (-first * GROUP) % LANES
        a, b = low, pltpu.roll(high, (by + three) % LANES, 1)
        if by:
            a = pltpu.roll(low, by, 1)
        ref[2 * WIDTH] = jnp.where(lane < three, a, b)

    at_low = rem_ref[1] == 0
    first = jnp.where(at_low, 0, NROW - WIDTH)
    by = jnp.where(at_low, NC - rem_ref[0], rem_ref[0])
    strips = jnp.zeros((5 * NZ, LANES), jnp.float32)
    for w in range(WIDTH):
        row = first + w
        main = xt_ref[row]
        moved = pltpu.roll(main, jnp.bitwise_and(by, NC - 1), 1)
        end_ref[2 * w] = moved[:, :LANES]
        end_ref[2 * w + 1] = moved[:, LANES:]
        above = pltpu.roll(high, jnp.bitwise_and(2 * LANES - GROUP * row - GROUP // 2, LANES - 1), 1)
        below = pltpu.roll(low, jnp.bitwise_and(2 * LANES - GROUP * row - GROUP // 2, LANES - 1), 1)
        wide = jnp.concatenate([main, above, below], axis=1)
        cut = pltpu.roll(wide, jnp.bitwise_and(by - (NC - GROUP // 2) + w * GROUP + 2 * NC, 2 * NC - 1), 1)
        strips = jnp.where(lane // GROUP == w, cut[:, :LANES], strips)
    end_ref[2 * WIDTH] = strips


def inner_kernel(xt_ref, strip_ref, out_ref, kept_ref, prim_ref, half_ref, prev_ref, first_ref, second_ref):
    cons = row_of(strip_ref)
    prim, speed, az = edge_faces_of(cons)
    keep_faces(first_ref, az)
    half = strip_half(cons, prim, speed, az, rolled(cons, GROUP, 1), rolled(cons, -GROUP, 1))
    keep_faces(second_ref, second_order_faces(primitive(half), 2, 1))
    predict(
        NROW,
        lambda i: row_of(xt_ref, i),
        lambda i: (first_ref, i),
        lambda i, arrays: put_row(prim_ref, i, arrays),
        half_ref,
        prev_ref,
    )
    for n in range(4):
        kept_ref[n] = prim_ref[1 + n]
        kept_ref[4 + n] = prim_ref[NROW - 5 + n]
    correct(
        NROW - 4,
        lambda i: row_of(prim_ref, i + 2),
        lambda i: row_of(xt_ref, i + 2),
        second_ref,
        lambda i: i + 2,
        lambda i, arrays: put_row(out_ref, i + 2, arrays),
        half_ref,
        prev_ref,
    )


def outer_kernel(
    rem_ref, xt_ref, strip_ref, kept_ref, up_ref, dn_ref, e1_ref, e2_ref, in_ref, out_ref,
    cons_ref, prim_ref, half_ref, prev_ref, first_ref, second_ref, ghost_ref, strips_ref,
):
    out_ref[pl.ds(WIDTH, NROW - 2 * WIDTH)] = in_ref[pl.ds(WIDTH, NROW - 2 * WIDTH)]
    rem, rad, last = rem_ref[0], rem_ref[1], rem_ref[2]
    lane = lanes_of((5 * NZ, LANES))
    three = WIDTH * GROUP

    def own_side(seg, ref):
        for w in range(WIDTH):
            for side in range(2):
                cons_ref[seg, WIDTH * seg + w, :, side * LANES : (side + 1) * LANES] = ref[2 * w + side]

    def end_side(seg, upper_ref, lower_ref, cut):
        for w in range(WIDTH):
            for side in range(2):
                cons_ref[seg, WIDTH * seg + w, :, side * LANES : (side + 1) * LANES] = jnp.where(
                    lane + side * LANES >= cut, upper_ref[2 * w + side], lower_ref[2 * w + side]
                )

    @pl.when(rad != 0)
    def _():
        own_side(0, up_ref)
        strips_ref[0] = up_ref[2 * WIDTH]
        strips_ref[1] = pltpu.roll(up_ref[2 * WIDTH], LANES - three, 1)

    @pl.when(rad == 0)
    def _():
        end_side(0, e1_ref, e2_ref, rem)
        strips_ref[0] = e2_ref[2 * WIDTH]
        strips_ref[1] = e1_ref[2 * WIDTH]

    @pl.when(rad != last)
    def _():
        own_side(1, dn_ref)
        strips_ref[0] = jnp.where(lane < three, strips_ref[0], pltpu.roll(dn_ref[2 * WIDTH], three, 1))
        strips_ref[1] = jnp.where(lane < three, strips_ref[1], dn_ref[2 * WIDTH])

    @pl.when(rad == last)
    def _():
        end_side(1, e2_ref, e1_ref, NC - rem)
        strips_ref[0] = jnp.where(lane < three, strips_ref[0], pltpu.roll(e1_ref[2 * WIDTH], three, 1))
        strips_ref[1] = jnp.where(lane < three, strips_ref[1], pltpu.roll(e2_ref[2 * WIDTH], three, 1))

    for w in range(WIDTH):
        cons_ref[0, WIDTH + w] = xt_ref[w]
        cons_ref[1, w] = xt_ref[NROW - WIDTH + w]
    for n in range(4):
        prim_ref[0, 3 + n] = kept_ref[n]
        prim_ref[1, n] = kept_ref[4 + n]

    ghost = [
        jnp.concatenate([strips_ref[0, pl.ds(c * NZ, NZ), :], strips_ref[1, pl.ds(c * NZ, NZ), :]], axis=1)
        for c in range(5)
    ]
    keep_faces(ghost_ref, edge_faces_of(ghost)[2])
    cons = row_of(strip_ref)
    prim, speed, az = edge_faces_of(cons)
    keep_faces(first_ref, az)
    in_tile = lanes_of((NZ, NC)) % LANES
    below = [
        jnp.where(in_tile < GROUP, a, b) for a, b in zip(rolled(ghost, -2 * GROUP, 1), rolled(cons, GROUP, 1))
    ]
    above = [
        jnp.where(in_tile >= LANES - GROUP, a, b)
        for a, b in zip(rolled(ghost, LANES - 4 * GROUP, 1), rolled(cons, -GROUP, 1))
    ]
    half = strip_half(cons, prim, speed, az, below, above)
    keep_faces(second_ref, second_order_faces(primitive(half), 2, 1))

    group = lanes_of((NZ, LANES)) // GROUP
    for side in range(2):
        for c in range(5):
            rows = pl.ds(c * NZ, NZ)
            mine = first_ref[side, rows, :]
            both = ghost_ref[side, rows, :]
            seg0 = jnp.where(group == 3, pltpu.roll(mine, 3 * GROUP, 1), both)
            seg1 = jnp.where(group == 1, pltpu.roll(mine, 2 * GROUP, 1), pltpu.roll(both, LANES - GROUP, 1))
            ghost_ref[side, rows, :] = seg0
            first_ref[side, rows, :] = seg1

    for seg in range(2):
        predict(
            5,
            lambda i: row_of(cons_ref, seg, i + seg),
            lambda i: ((ghost_ref, first_ref)[seg], i),
            lambda i, arrays: put_row(prim_ref.at[seg], i - 1 + 4 * seg, arrays),
            half_ref,
            prev_ref,
        )
        correct(
            5,
            lambda i: row_of(prim_ref, seg, i + 1),
            lambda i: row_of(cons_ref, seg, i + 2 - 3 * seg),
            second_ref,
            lambda i: i - 1 if seg == 0 else i + NROW - 4,
            lambda i, arrays: put_row(out_ref, i - 1 if seg == 0 else i + NROW - 4, arrays),
            half_ref,
            prev_ref,
        )


def remap_kernel(count, shift_ref, frac_ref, x_ref, o_ref, held_ref):
    row = shift_ref[NROW]
    shift, frac = shift_ref[row], frac_ref[row]
    hop = jnp.bitwise_and(jnp.right_shift(shift, 8), count - 1)
    rem = jnp.bitwise_and(shift, NC - 1)
    lane = lanes_of((5 * NZ, NC))

    def one(m, carry):
        here = jnp.bitwise_and(m + count - 1, count - 1)
        before = jnp.bitwise_and(m + count - 2, count - 1)
        block = x_ref[here]
        lower = jnp.where(lane == 0, pltpu.roll(x_ref[before], 1, 1), pltpu.roll(block, 1, 1))
        moved = pltpu.roll((1.0 - frac) * block + frac * lower, rem, 1)

        @pl.when(m > 0)
        def _():
            o_ref[jnp.bitwise_and(m + hop + count - 1, count - 1)] = jnp.where(lane >= rem, moved, held_ref[...])

        held_ref[...] = moved
        return carry

    lax.fori_loop(0, count + 1, one, 0)


def finish_kernel(y_ref, o_ref):
    for c in range(5):
        o_ref[pl.ds(c * NZ, NZ)] = jnp.swapaxes(y_ref[:, pl.ds(c * NZ, NZ), :], 0, 1)


def shape(*dims):
    return jax.ShapeDtypeStruct(dims, jnp.float32)


def local(conserved, shift_cells, shift_frac, boundary_offset):
    azs, rads = lax.axis_size("az"), lax.axis_size("rad")
    az, rad = lax.axis_index("az"), lax.axis_index("rad")
    offset = boundary_offset[0]
    hop, rem = offset // NC, offset % NC
    scalars = jnp.stack([rem, rad, jnp.int32(rads - 1)]).astype(jnp.int32)
    row_shape, strip_shape = (5 * NZ, NC), (5 * NZ, LANES)
    rows, own = pl.pallas_call(
        prep_kernel,
        out_shape=(shape(NROW, *row_shape), shape(*strip_shape)),
        in_specs=[VMEM],
        out_specs=(VMEM,) * 2,
        compiler_params=PARAMS,
    )(conserved.reshape(5 * NZ, NROW, NC))
    left = lax.ppermute(own, "az", [(i, (i + 1) % azs) for i in range(azs)])
    right = lax.ppermute(own, "az", [((i + 1) % azs, i) for i in range(azs)])
    rim = shape(2 * WIDTH + 1, *strip_shape)
    strip, up, dn, end = pl.pallas_call(
        rims_kernel,
        out_shape=(shape(*row_shape), rim, rim, rim),
        in_specs=[SMEM] + [VMEM] * 4,
        out_specs=(VMEM,) * 4,
        compiler_params=PARAMS,
    )(scalars, rows, own, left, right)
    from_below = lax.ppermute(up, "rad", [(i, i + 1) for i in range(rads - 1)])
    from_above = lax.ppermute(dn, "rad", [(i + 1, i) for i in range(rads - 1)])

    scratch = [
        pltpu.VMEM((1, *row_shape), jnp.float32),
        pltpu.VMEM((2, *row_shape), jnp.float32),
        pltpu.VMEM((2, *strip_shape), jnp.float32),
        pltpu.VMEM((2, *strip_shape), jnp.float32),
    ]

    def inner(rows, strip):
        return pl.pallas_call(
            inner_kernel,
            out_shape=(shape(NROW, *row_shape), shape(8, *row_shape)),
            in_specs=[VMEM] * 2,
            out_specs=(VMEM,) * 2,
            scratch_shapes=[pltpu.VMEM((NROW, *row_shape), jnp.float32), *scratch],
            compiler_params=PARAMS,
            cost_estimate=pl.CostEstimate(flops=30 * 10**6, bytes_accessed=4 * 2**20, transcendentals=0),
        )(rows, strip)

    def ends(k):
        pairs = [(a * rads + rads - 1, (a + k) % azs * rads) for a in range(azs)]
        return pairs + [(b, a) for a, b in pairs]

    def moved_by(k):
        def send(block, rows, strip):
            first, second = (lax.ppermute(block, ("az", "rad"), ends(j % azs)) for j in (k, k + 1))
            return first, second, *inner(rows, strip)

        return send

    first, second, updated, kept = lax.switch(hop, [moved_by(k) for k in range(azs)], end, rows, strip)
    updated = pl.pallas_call(
        outer_kernel,
        out_shape=shape(NROW, *row_shape),
        in_specs=[SMEM] + [VMEM] * 8,
        out_specs=VMEM,
        scratch_shapes=[
            pltpu.VMEM((2, 6, *row_shape), jnp.float32),
            pltpu.VMEM((2, 7, *row_shape), jnp.float32),
            *scratch,
            pltpu.VMEM((2, *strip_shape), jnp.float32),
            pltpu.VMEM((2, *strip_shape), jnp.float32),
        ],
        compiler_params=PARAMS,
    )(scalars, rows, strip, kept, from_below, from_above, first, second, updated)

    whole_row = lax.all_to_all(updated, "az", 0, 0, tiled=True)
    shifts = jnp.concatenate([shift_cells, az[None].astype(jnp.int32)])
    moved = pl.pallas_call(
        functools.partial(remap_kernel, azs),
        out_shape=shape(azs, *row_shape),
        in_specs=[SMEM, SMEM, VMEM],
        out_specs=VMEM,
        scratch_shapes=[pltpu.VMEM(row_shape, jnp.float32)],
        compiler_params=PARAMS,
    )(shifts, shift_frac, whole_row)
    back = lax.all_to_all(moved, "az", 0, 0, tiled=True)
    result = pl.pallas_call(
        finish_kernel,
        out_shape=shape(5 * NZ, NROW, NC),
        in_specs=[VMEM],
        out_specs=VMEM,
        compiler_params=PARAMS,
    )(back)
    return result.reshape(5, NZ, NROW, NC)


def solution(mesh):
    in_specs = (P(None, None, "rad", "az"), P("rad"), P("rad"), P())
    out_specs = P(None, None, "rad", "az")
    return jax.shard_map(local, mesh=mesh, in_specs=in_specs, out_specs=out_specs, check_vma=False)
```

time: 112 us -> 103 us (0.920)
  waiting for transfers between devices: 31.4 us -> 24.4 us
  starting transfers between devices: 31.6 us -> 27.6 us
  Pallas kernels: 22.8 us -> 25.4 us
    ppermute x2, waiting for transfers between devices: 8.87 us -> 0.01 us  [send(): lax.ppermute(block, ('az', 'rad'), ends(j % azs))]
    ppermute x2, starting transfers between devices: 11.9 us -> 7.8 us  [send(): lax.ppermute(block, ('az', 'rad'), ends(j % azs))]
    pallas_call x3 -> x4, Pallas kernels: 17.6 us -> 20.2 us  [the longest x1 10.3 us: inner(): pl.pallas_call(inner_kernel, out_shape=(shape(NROW, *row_shape), shape(8,...]
    ppermute x4, waiting for transfers between devices: 2.49 us -> 4.3 us  [the longest x1 3.44 us: local(): left = lax.ppermute(own, 'az', [(i, (i + 1) % azs) for i in range(azs)])]
  transfers between devices with their start and end apart: 7 -> 7, of which waited for: 5 -> 3; matrix products, arithmetic and copies ran while one was open for 0% -> 0% of each run, Pallas kernels for 0% -> 10%
where the time goes in v1:
time: 103 us
  starting transfers between devices  27.6 us (27%)
  Pallas kernels  25.4 us (25%)
  waiting for transfers between devices  24.4 us (24%)
  blocking collectives  23.1 us (22%)
  local copies, waits for them, and re-layouts  1.32 us (1%)
    all_to_all x1, blocking collectives, local(): back = lax.all_to_all(moved, 'az', 0, 0, tiled=True)  23.1 us
    all_to_all x1, waiting for transfers between devices, local(): whole_row = lax.all_to_all(updated, 'az', 0, 0, tiled=True)  20.1 us
    all_to_all x1, starting transfers between devices, local(): whole_row = lax.all_to_all(updated, 'az', 0, 0, tiled=True)  12.5 us
    pallas_call x1, Pallas kernels, inner(): pl.pallas_call(inner_kernel, out_shape=(shape(NROW, *row_shape), shape(8,...  10.3 us
    pallas_call x1, Pallas kernels, local(): pl.pallas_call(outer_kernel, out_shape=shape(NROW, *row_shape), in_specs=...  8.29 us
    ppermute x2, starting transfers between devices, send(): lax.ppermute(block, ('az', 'rad'), ends(j % azs))  7.8 us
    pallas_call x1, Pallas kernels, local(): pl.pallas_call(functools.partial(remap_kernel, azs), out_shape=shape(azs,...  3.9 us
    ppermute x1, waiting for transfers between devices, local(): left = lax.ppermute(own, 'az', [(i, (i + 1) % azs) for i in range(azs)])  3.44 us
  transfers between devices with their start and end apart: 7, of which 3 were waited for; matrix products, arithmetic and copies ran while one was open for 0% of the time, Pallas kernels for 10%

profile of v1, /device:TPU:1, one launch (start us, length us, event | category | flops | bytes accessed | tf_op | source)
XLA Modules:
  0.0 102.9 jit_solution(9220765836132239351)
XLA Ops:
  0.0 0.0 copy-start
  0.0 1.3 %copy-done = f32[5,16,16,256]{3,2,1,0:T(8,128)S(1)} copy-done((f32[5,16,16,256]{3,2,1,0:T(8,128)S(1)}, f32[5,16,16,256]{3,2,1,0:T(8,128)}, u32[]{:S(2)}) %copy-start) | copy-done | bytes 1310744
  1.3 0.6 shard_map.46
  1.9 1.5 %collective-permute-start.33 = (f32[80,128]{1,0:T(8,128)S(1)}, f32[80,128]{1,0:T(8,128)S(1)}, u32[]{:S(2)}, u32[]{:S(2)}) collective-permute-start(f32[80,128]{1,0:T(8,128)S(1)} %get-tuple-element.192.own_ref), channel_id=1, source_target_pairs={{8,0},{16,8},{24,16},{32,24},{40,32},{48,40},{56,48},{64,56},{72,6... | collective-permute-start | bytes 122888 | tf_op jit(solution)/shard_map/ppermute | solution.py:470
  3.4 1.3 %collective-permute-start.32 = (f32[80,128]{1,0:T(8,128)S(1)}, f32[80,128]{1,0:T(8,128)S(1)}, u32[]{:S(2)}, u32[]{:S(2)}) collective-permute-start(f32[80,128]{1,0:T(8,128)S(1)} %get-tuple-element.192.own_ref), channel_id=1, source_target_pairs={{0,8},{8,16},{16,24},{24,32},{32,40},{40,48},{48,56},{56,64},{64,7... | collective-permute-start | bytes 122888 | tf_op jit(solution)/shard_map/ppermute | solution.py:469
  5.3 0.1 pad_add_fusion.1.rem_ref
  5.4 0.9 collective-permute-done.33.right_ref
  6.3 3.4 %collective-permute-done.32.left_ref = f32[80,128]{1,0:T(8,128)S(1)} collective-permute-done((f32[80,128]{1,0:T(8,128)S(1)}, f32[80,128]{1,0:T(8,128)S(1)}, u32[]{:S(2)}, u32[]{:S(2)}) %collective-permute-start.32) | collective-permute-done | bytes 40992 | tf_op jit(solution)/shard_map/ppermute | solution.py:469
  9.7 1.0 shard_map.47
  10.7 3.2 %collective-permute-start.34 = (f32[7,80,128]{2,1,0:T(8,128)S(1)}, f32[7,80,128]{2,1,0:T(8,128)S(1)}, u32[]{:S(2)}, u32[]{:S(2)}) collective-permute-start(f32[7,80,128]{2,1,0:T(8,128)S(1)} %get-tuple-element.196), channel_id=1, source_target_pairs={{0,1},{1,2},{2,3},{3,4},{4,5},{5,6},{6,7},{8,9},{9,10},{10,11},{11... | collective-permute-start | bytes 860168 | tf_op jit(solution)/shard_map/ppermute | solution.py:479
  13.9 1.3 %collective-permute-start.35 = (f32[7,80,128]{2,1,0:T(8,128)S(1)}, f32[7,80,128]{2,1,0:T(8,128)S(1)}, u32[]{:S(2)}, u32[]{:S(2)}) collective-permute-start(f32[7,80,128]{2,1,0:T(8,128)S(1)} %get-tuple-element.197), channel_id=1, source_target_pairs={{1,0},{2,1},{3,2},{4,3},{5,4},{6,5},{7,6},{9,8},{10,9},{11,10},{12... | collective-permute-start | bytes 860168 | tf_op jit(solution)/shard_map/ppermute | solution.py:480
  15.2 18.4 %conditional.1 = (f32[7,80,128]{2,1,0:T(8,128)}, f32[7,80,128]{2,1,0:T(8,128)}, f32[16,80,256]{2,1,0:T(8,128)}, f32[8,80,256]{2,1,0:T(8,128)S(1)}) conditional(s32[]{:T(128)} %clamp.3, (f32[7,80,128]{2,1,0:T(8,128)S(1)}, f32[16,80,256]{2,1,0:T(8,128)S(1)}, f32[80,256]{1,0:T(8,128)S(1)}) %tuple.69, ...), branch_computations={%region_0.1_spmd, %region_1.2_spmd, %region_2.3_spmd, %region_3.4_... | conditional | flops 30000000 | bytes 6488176 | solution.py:511
  15.5 5.9 %collective-permute-start.31 = (f32[7,80,128]{2,1,0:T(8,128)S(1)}, f32[7,80,128]{2,1,0:T(8,128)}, u32[]{:S(2)}, u32[]{:S(2)}) collective-permute-start(f32[7,80,128]{2,1,0:T(8,128)S(1)} %get-tuple-element.176), channel_id=1, source_target_pairs={{7,0},{15,8},{23,16},{31,24},{39,32},{47,40},{55,48},{63,56},{71,6... | collective-permute-start | bytes 860168 | tf_op jit(solution)/shard_map/cond/branch_15_fun/ppermute | solution.py:506
  21.4 1.9 %collective-permute-start.30 = (f32[7,80,128]{2,1,0:T(8,128)S(1)}, f32[7,80,128]{2,1,0:T(8,128)}, u32[]{:S(2)}, u32[]{:S(2)}) collective-permute-start(f32[7,80,128]{2,1,0:T(8,128)S(1)} %get-tuple-element.176), channel_id=1, source_target_pairs={{7,120},{15,0},{23,8},{31,16},{39,24},{47,32},{55,40},{63,48},{71,... | collective-permute-start | bytes 860168 | tf_op jit(solution)/shard_map/cond/branch_15_fun/ppermute | solution.py:506
  23.3 10.3 %branch_15_fun.1 = (f32[16,80,256]{2,1,0:T(8,128)}, f32[8,80,256]{2,1,0:T(8,128)S(1)}) custom-call(f32[16,80,256]{2,1,0:T(8,128)S(1)} %get-tuple-element.177.xt_ref, f32[80,256]{1,0:T(8,128)S(1)} %get-tuple-element.178.strip_ref), custom_call_target="tpu_custom_call" | custom-call | flops 30000000 | bytes 4194304 | tf_op jit(solution)/shard_map/cond/branch_15_fun/pallas_call | solution.py:490
  33.6 0.0 collective-permute-done.31
  33.6 0.0 collective-permute-done.30
  33.6 0.0 collective-permute-done.34.up_ref
  33.6 0.0 collective-permute-done.35.dn_ref
  33.6 8.3 %shard_map.48 = f32[16,80,256]{2,1,0:T(8,128)} custom-call(s32[3]{0:T(128)S(1)} %pad_add_fusion.1.rem_ref, f32[16,80,256]{2,1,0:T(8,128)S(1)} %get-tuple-element.191.xt_ref, f32[80,256]{1,0:T(8,128)S(1)} %get-tuple-element.193.strip_ref, f32[8,80,256]{2,1,0:T(8,128)S(1)} %get-tuple-element.195.kept_ref, f32[7,80,128]{2,1,0:T(8,128)S(1)} %collective-permute-done.34.up_ref, ...), custom_call_target="tpu_custom_call" | custom-call | tf_op jit(solution)/shard_map/pallas_call | solution.py:512
  41.9 0.0 copy-start.2
  41.9 0.0 copy-start.1
  41.9 12.5 %all-to-all-start = ((f32[16,80,256]{2,1,0:T(8,128)}), f32[16,80,256]{2,1,0:T(8,128)S(1)}, u32[]{:S(2)}, u32[]{:S(2)}) async-start(f32[16,80,256]{2,1,0:T(8,128)} %shard_map.48), calls=%async_computation | async-start | bytes 2621440 | tf_op jit(solution)/shard_map/all_to_all | solution.py:527
  54.4 0.0 copy-done.2
  54.4 0.1 pad_add_fusion.shift_ref
  54.5 20.1 %all-to-all-done.x_ref = f32[16,80,256]{2,1,0:T(8,128)S(1)} async-done(((f32[16,80,256]{2,1,0:T(8,128)}), f32[16,80,256]{2,1,0:T(8,128)S(1)}, u32[]{:S(2)}, u32[]{:S(2)}) %all-to-all-start) | async-done | bytes 1310752 | tf_op jit(solution)/shard_map/all_to_all | solution.py:527
  74.6 0.0 copy-done.1
  74.6 3.9 %shard_map.49 = f32[16,80,256]{2,1,0:T(8,128)S(1)} custom-call(s32[17]{0:T(128)S(1)} %pad_add_fusion.shift_ref, f32[16]{0:T(128)S(1)} %copy-done.1, f32[16,80,256]{2,1,0:T(8,128)S(1)} %all-to-all-done.x_ref), custom_call_target="tpu_custom_call" | custom-call | tf_op jit(solution)/shard_map/pallas_call | solution.py:529
  78.5 23.1 %all_to_all.10.y_ref = f32[16,80,256]{2,1,0:T(8,128)S(1)} all-to-all(f32[16,80,256]{2,1,0:T(8,128)S(1)} %shard_map.49), channel_id=1, replica_groups=mesh['az'=16,'rad'=8] {'az'}, dimensions={0} | all-to-all | bytes 2621440 | tf_op jit(solution)/shard_map/all_to_all | solution.py:537
  101.6 1.3 %shard_map.50 = f32[80,16,256]{2,1,0:T(8,128)} custom-call(f32[16,80,256]{2,1,0:T(8,128)S(1)} %all_to_all.10.y_ref), custom_call_target="tpu_custom_call" | custom-call | tf_op jit(solution)/shard_map/pallas_call | solution.py:538
Async XLA Ops:
  0.0 1.3 %copy-start = (f32[5,16,16,256]{3,2,1,0:T(8,128)S(1)}, f32[5,16,16,256]{3,2,1,0:T(8,128)}, u32[]{:S(2)}) copy-start(f32[5,16,16,256]{3,2,1,0:T(8,128)} %param.20) | copy-start | bytes 3932164
  1.9 4.4 %collective-permute-start.33 = (f32[80,128]{1,0:T(8,128)S(1)}, f32[80,128]{1,0:T(8,128)S(1)}, u32[]{:S(2)}, u32[]{:S(2)}) collective-permute-start(f32[80,128]{1,0:T(8,128)S(1)} %get-tuple-element.192.own_ref), channel_id=1, source_target_pairs={{8,0},{16,8},{24,16},{32,24},{40,32},{48,40},{56,48},{64,56},{72,6... | collective-permute-start | bytes 122888 | tf_op jit(solution)/shard_map/ppermute | solution.py:470
  3.4 6.3 %collective-permute-start.32 = (f32[80,128]{1,0:T(8,128)S(1)}, f32[80,128]{1,0:T(8,128)S(1)}, u32[]{:S(2)}, u32[]{:S(2)}) collective-permute-start(f32[80,128]{1,0:T(8,128)S(1)} %get-tuple-element.192.own_ref), channel_id=1, source_target_pairs={{0,8},{8,16},{16,24},{24,32},{32,40},{40,48},{48,56},{56,64},{64,7... | collective-permute-start | bytes 122888 | tf_op jit(solution)/shard_map/ppermute | solution.py:469
  10.7 22.9 %collective-permute-start.34 = (f32[7,80,128]{2,1,0:T(8,128)S(1)}, f32[7,80,128]{2,1,0:T(8,128)S(1)}, u32[]{:S(2)}, u32[]{:S(2)}) collective-permute-start(f32[7,80,128]{2,1,0:T(8,128)S(1)} %get-tuple-element.196), channel_id=1, source_target_pairs={{0,1},{1,2},{2,3},{3,4},{4,5},{5,6},{6,7},{8,9},{9,10},{10,11},{11... | collective-permute-start | bytes 860168 | tf_op jit(solution)/shard_map/ppermute | solution.py:479
  13.9 19.7 %collective-permute-start.35 = (f32[7,80,128]{2,1,0:T(8,128)S(1)}, f32[7,80,128]{2,1,0:T(8,128)S(1)}, u32[]{:S(2)}, u32[]{:S(2)}) collective-permute-start(f32[7,80,128]{2,1,0:T(8,128)S(1)} %get-tuple-element.197), channel_id=1, source_target_pairs={{1,0},{2,1},{3,2},{4,3},{5,4},{6,5},{7,6},{9,8},{10,9},{11,10},{12... | collective-permute-start | bytes 860168 | tf_op jit(solution)/shard_map/ppermute | solution.py:480
  15.5 18.1 %collective-permute-start.31 = (f32[7,80,128]{2,1,0:T(8,128)S(1)}, f32[7,80,128]{2,1,0:T(8,128)}, u32[]{:S(2)}, u32[]{:S(2)}) collective-permute-start(f32[7,80,128]{2,1,0:T(8,128)S(1)} %get-tuple-element.176), channel_id=1, source_target_pairs={{7,0},{15,8},{23,16},{31,24},{39,32},{47,40},{55,48},{63,56},{71,6... | collective-permute-start | bytes 860168 | tf_op jit(solution)/shard_map/cond/branch_15_fun/ppermute | solution.py:506
  21.4 12.2 %collective-permute-start.30 = (f32[7,80,128]{2,1,0:T(8,128)S(1)}, f32[7,80,128]{2,1,0:T(8,128)}, u32[]{:S(2)}, u32[]{:S(2)}) collective-permute-start(f32[7,80,128]{2,1,0:T(8,128)S(1)} %get-tuple-element.176), channel_id=1, source_target_pairs={{7,120},{15,0},{23,8},{31,16},{39,24},{47,32},{55,40},{63,48},{71,... | collective-permute-start | bytes 860168 | tf_op jit(solution)/shard_map/cond/branch_15_fun/ppermute | solution.py:506
  41.9 12.5 %copy-start.2 = (s32[16]{0:T(128)S(1)}, s32[16]{0:T(128)}, u32[]{:S(2)}) copy-start(s32[16]{0:T(128)} %param.21) | copy-start | bytes 196
  41.9 32.7 %copy-start.1 = (f32[16]{0:T(128)S(1)}, f32[16]{0:T(128)}, u32[]{:S(2)}) copy-start(f32[16]{0:T(128)} %frac_ref.1) | copy-start | bytes 196
  41.9 32.7 %all-to-all-start = ((f32[16,80,256]{2,1,0:T(8,128)}), f32[16,80,256]{2,1,0:T(8,128)S(1)}, u32[]{:S(2)}, u32[]{:S(2)}) async-start(f32[16,80,256]{2,1,0:T(8,128)} %shard_map.48), calls=%async_computation | async-start | bytes 2621440 | tf_op jit(solution)/shard_map/all_to_all | solution.py:527

commit v2 on v1

--- a/solution.py
+++ b/solution.py
@@ -21,6 +21,7 @@
 CORR = 0.5 * step_ratio
 GROUP = 8
 VMEM = pl.BlockSpec(memory_space=pltpu.VMEM)
+ANY = pl.BlockSpec(memory_space=pl.ANY)
 SMEM = pl.BlockSpec(memory_space=pltpu.SMEM)
 PARAMS = pltpu.CompilerParams(vmem_limit_bytes=48 * 2**20)
 
@@ -170,73 +171,89 @@
     return lower, upper
 
 
-def predict(count, load, faces_at, sink, half_ref, prev_ref):
-    def step(i, carry):
+def predict(count, load, faces_at, sink, save_ref, unroll):
+    def state(i):
         cons = load(i)
         prim = primitive(cons)
         speed = sound(prim)
-        flux = flux_of(prim, cons, 1)
-        reach = jnp.abs(prim[1]) + speed
-
-        @pl.when(i > 0)
-        def _():
-            low_reach = prev_ref[1, pl.ds(0, NZ), :]
-            rad = twice_face(row_of(prev_ref, 0), load(i - 1), low_reach, flux, cons, reach)
-
-            @pl.when(i > 1)
-            def _():
-                sink(i - 1, primitive([x - PRED * y for x, y in zip(row_of(half_ref, 0), rad)]))
-
-            @pl.when(i < count - 1)
-            def _():
-                lower, upper = patched(first_order_faces(prim, cons, speed, 2, 1), *faces_at(i), 1)
-                vert = first_order_faces(prim, cons, speed, 3, 0)
-                source = added_sources(cons, prim)
-                for c in range(5):
-                    total = (upper[c] - lower[c]) + (pltpu.roll(vert[c], NZ - 1, 0) - vert[c]) - rad[c]
-                    value = cons[c] - PRED * total
-                    if c in source:
-                        value = value + 0.5 * step_ratio * source[c]
-                    half_ref[0, pl.ds(c * NZ, NZ), :] = value
-
-        put_row(prev_ref, 0, flux)
-        prev_ref[1, pl.ds(0, NZ), :] = reach
+        return cons, prim, speed, (flux_of(prim, cons, 1), cons, jnp.abs(prim[1]) + speed)
+
+    def keep(prim, speed, rad_state, rad):
+        put_row(save_ref, 0, rad_state[0])
+        put_row(save_ref, 1, rad)
+        put_row(save_ref, 2, prim)
+        save_ref[3, pl.ds(0, NZ), :] = speed
+        save_ref[3, pl.ds(NZ, NZ), :] = rad_state[2]
+
+    _, _, _, before = state(0)
+    _, prim, speed, here = state(1)
+    keep(prim, speed, here, twice_face(*before, *here))
+
+    def step(i, carry):
+        cons = load(i)
+        low = row_of(save_ref, 1)
+        prim = row_of(save_ref, 2)
+        speed = save_ref[3, pl.ds(0, NZ), :]
+        here = (row_of(save_ref, 0), cons, save_ref[3, pl.ds(NZ, NZ), :])
+        _, next_prim, next_speed, there = state(i + 1)
+        rad = twice_face(*here, *there)
+        keep(next_prim, next_speed, there, rad)
+        total = [x - y for x, y in zip(rad, low)]
+        vert = first_order_faces(prim, cons, speed, 3, 0)
+        total = [t + (pltpu.roll(x, NZ - 1, 0) - x) for t, x in zip(total, vert)]
+        lower, upper = patched(first_order_faces(prim, cons, speed, 2, 1), *faces_at(i), 1)
+        source = added_sources(cons, prim)
+        half = []
+        for c in range(5):
+            value = cons[c] - PRED * (total[c] + (upper[c] - lower[c]))
+            half.append(value + 0.5 * step_ratio * source[c] if c in source else value)
+        sink(i, primitive(half))
         return carry
 
-    lax.fori_loop(0, count, step, 0)
-
-
-def correct(count, load, cons_at, faces_ref, group_of, sink, half_ref, prev_ref):
-    def step(i, carry):
+    lax.fori_loop(1, count - 1, step, 0, unroll=unroll)
+
+
+def correct(count, load, cons_at, faces_ref, group_of, sink, save_ref, unroll):
+    def sides(i):
         prim = load(i)
         half_slope = [0.5 * minmod(x - a, b - x) for x, a, b in zip(prim, load(i - 1), load(i + 1))]
-        high = [x - s for x, s in zip(prim, half_slope)]
-
-        @pl.when(i > 0)
-        def _():
-            rad = twice_face(*state_at(row_of(prev_ref, 0), 1), *state_at(high, 1))
-
-            @pl.when(i > 1)
-            def _():
-                sink(i - 1, [x - CORR * y for x, y in zip(row_of(half_ref, 0), rad)])
-
-            @pl.when(i < count - 1)
-            def _():
-                lower, upper = patched(second_order_faces(prim, 2, 1), faces_ref, group_of(i), 2)
-                vert = second_order_faces(prim, 3, 0)
-                source = added_sources(conserved_of(prim), prim)
-                cons = cons_at(i)
-                for c in range(5):
-                    total = (upper[c] - lower[c]) + (pltpu.roll(vert[c], NZ - 1, 0) - vert[c]) - rad[c]
-                    value = cons[c] - CORR * total
-                    if c in source:
-                        value = value + step_ratio * source[c]
-                    half_ref[0, pl.ds(c * NZ, NZ), :] = value
-
-        put_row(prev_ref, 0, [x + s for x, s in zip(prim, half_slope)])
+        return [x - s for x, s in zip(prim, half_slope)], [x + s for x, s in zip(prim, half_slope)]
+
+    _, above = sides(0)
+    high, upper_side = sides(1)
+    put_row(save_ref, 0, upper_side)
+    put_row(save_ref, 1, twice_face(*state_at(above, 1), *state_at(high, 1)))
+
+    def step(i, carry):
+        below = row_of(save_ref, 0)
+        low = row_of(save_ref, 1)
+        high, upper_side = sides(i + 1)
+        rad = twice_face(*state_at(below, 1), *state_at(high, 1))
+        put_row(save_ref, 0, upper_side)
+        put_row(save_ref, 1, rad)
+        total = [x - y for x, y in zip(rad, low)]
+        prim = load(i)
+        vert = second_order_faces(prim, 3, 0)
+        total = [t + (pltpu.roll(x, NZ - 1, 0) - x) for t, x in zip(total, vert)]
+        lower, upper = patched(second_order_faces(prim, 2, 1), faces_ref, group_of(i), 2)
+        source = added_sources(conserved_of(prim), prim)
+        cons = cons_at(i)
+        done = []
+        for c in range(5):
+            value = cons[c] - CORR * (total[c] + (upper[c] - lower[c]))
+            done.append(value + step_ratio * source[c] if c in source else value)
+        sink(i, done)
         return carry
 
-    lax.fori_loop(0, count, step, 0)
+    lax.fori_loop(1, count - 1, step, 0, unroll=unroll)
+
+
+def loop_scratch():
+    return [
+        pltpu.VMEM((4, 5 * NZ, NC), jnp.float32),
+        pltpu.VMEM((2, 5 * NZ, LANES), jnp.float32),
+        pltpu.VMEM((2, 5 * NZ, LANES), jnp.float32),
+    ]
 
 
 def prep_kernel(x_ref, xt_ref, own_ref):
@@ -287,7 +304,7 @@
     end_ref[2 * WIDTH] = strips
 
 
-def inner_kernel(xt_ref, strip_ref, out_ref, kept_ref, prim_ref, half_ref, prev_ref, first_ref, second_ref):
+def inner_kernel(xt_ref, strip_ref, out_ref, kept_ref, prim_ref, save_ref, first_ref, second_ref):
     cons = row_of(strip_ref)
     prim, speed, az = edge_faces_of(cons)
     keep_faces(first_ref, az)
@@ -298,8 +315,8 @@
         lambda i: row_of(xt_ref, i),
         lambda i: (first_ref, i),
         lambda i, arrays: put_row(prim_ref, i, arrays),
-        half_ref,
-        prev_ref,
+        save_ref,
+        2,
     )
     for n in range(4):
         kept_ref[n] = prim_ref[1 + n]
@@ -311,16 +328,17 @@
         second_ref,
         lambda i: i + 2,
         lambda i, arrays: put_row(out_ref, i + 2, arrays),
-        half_ref,
-        prev_ref,
+        save_ref,
+        2,
     )
 
 
 def outer_kernel(
-    rem_ref, xt_ref, strip_ref, kept_ref, up_ref, dn_ref, e1_ref, e2_ref, in_ref, out_ref,
-    cons_ref, prim_ref, half_ref, prev_ref, first_ref, second_ref, ghost_ref, strips_ref,
+    rem_ref, xt_ref, strip_ref, kept_ref, up_ref, dn_ref, e1_ref, e2_ref, seen_ref, in_ref, whole_ref,
+    cons_ref, prim_ref, save_ref, first_ref, second_ref, ghost_ref, strips_ref,
+    out_ref, sem,
 ):
-    out_ref[pl.ds(WIDTH, NROW - 2 * WIDTH)] = in_ref[pl.ds(WIDTH, NROW - 2 * WIDTH)]
+    del seen_ref, in_ref
     rem, rad, last = rem_ref[0], rem_ref[1], rem_ref[2]
     lane = lanes_of((5 * NZ, LANES))
     three = WIDTH * GROUP
@@ -372,7 +390,7 @@
         jnp.concatenate([strips_ref[0, pl.ds(c * NZ, NZ), :], strips_ref[1, pl.ds(c * NZ, NZ), :]], axis=1)
         for c in range(5)
     ]
-    keep_faces(ghost_ref, edge_faces_of(ghost)[2])
+    keep_faces(ghost_ref.at[0], edge_faces_of(ghost)[2])
     cons = row_of(strip_ref)
     prim, speed, az = edge_faces_of(cons)
     keep_faces(first_ref, az)
@@ -387,60 +405,69 @@
     half = strip_half(cons, prim, speed, az, below, above)
     keep_faces(second_ref, second_order_faces(primitive(half), 2, 1))
 
-    group = lanes_of((NZ, LANES)) // GROUP
+    group = lanes_of((5 * NZ, LANES)) // GROUP
     for side in range(2):
-        for c in range(5):
-            rows = pl.ds(c * NZ, NZ)
-            mine = first_ref[side, rows, :]
-            both = ghost_ref[side, rows, :]
-            seg0 = jnp.where(group == 3, pltpu.roll(mine, 3 * GROUP, 1), both)
-            seg1 = jnp.where(group == 1, pltpu.roll(mine, 2 * GROUP, 1), pltpu.roll(both, LANES - GROUP, 1))
-            ghost_ref[side, rows, :] = seg0
-            first_ref[side, rows, :] = seg1
-
-    for seg in range(2):
+        mine, both = first_ref[side], ghost_ref[0, side]
+        ghost_ref[0, side] = jnp.where(group == 3, pltpu.roll(mine, 3 * GROUP, 1), both)
+        ghost_ref[1, side] = jnp.where(group == 1, pltpu.roll(mine, 2 * GROUP, 1), pltpu.roll(both, LANES - GROUP, 1))
+
+    def segment(seg, carry):
         predict(
             5,
             lambda i: row_of(cons_ref, seg, i + seg),
-            lambda i: ((ghost_ref, first_ref)[seg], i),
+            lambda i: (ghost_ref.at[seg], i),
             lambda i, arrays: put_row(prim_ref.at[seg], i - 1 + 4 * seg, arrays),
-            half_ref,
-            prev_ref,
+            save_ref,
+            1,
         )
         correct(
             5,
             lambda i: row_of(prim_ref, seg, i + 1),
             lambda i: row_of(cons_ref, seg, i + 2 - 3 * seg),
             second_ref,
-            lambda i: i - 1 if seg == 0 else i + NROW - 4,
-            lambda i, arrays: put_row(out_ref, i - 1 if seg == 0 else i + NROW - 4, arrays),
-            half_ref,
-            prev_ref,
+            lambda i: i - 1 + 13 * seg,
+            lambda i, arrays: put_row(out_ref.at[seg], i - 1, arrays),
+            save_ref,
+            1,
         )
-
-
-def remap_kernel(count, shift_ref, frac_ref, x_ref, o_ref, held_ref):
+        return carry
+
+    lax.fori_loop(0, 2, segment, 0)
+    copies = [
+        pltpu.make_async_copy(out_ref.at[seg], whole_ref.at[pl.ds(seg * (NROW - WIDTH), WIDTH)], sem.at[seg])
+        for seg in range(2)
+    ]
+    for copy in copies:
+        copy.start()
+    for copy in copies:
+        copy.wait()
+
+
+def remap_kernel(count, shift_ref, frac_ref, x_ref, o_ref):
     row = shift_ref[NROW]
     shift, frac = shift_ref[row], frac_ref[row]
-    hop = jnp.bitwise_and(jnp.right_shift(shift, 8), count - 1)
-    rem = jnp.bitwise_and(shift, NC - 1)
-    lane = lanes_of((5 * NZ, NC))
-
-    def one(m, carry):
-        here = jnp.bitwise_and(m + count - 1, count - 1)
-        before = jnp.bitwise_and(m + count - 2, count - 1)
-        block = x_ref[here]
-        lower = jnp.where(lane == 0, pltpu.roll(x_ref[before], 1, 1), pltpu.roll(block, 1, 1))
-        moved = pltpu.roll((1.0 - frac) * block + frac * lower, rem, 1)
-
-        @pl.when(m > 0)
-        def _():
-            o_ref[jnp.bitwise_and(m + hop + count - 1, count - 1)] = jnp.where(lane >= rem, moved, held_ref[...])
-
-        held_ref[...] = moved
-        return carry
-
-    lax.fori_loop(0, count + 1, one, 0)
+    tiles = 2 * count
+    hop = jnp.bitwise_and(jnp.right_shift(shift, 7), tiles - 1)
+    rem = jnp.bitwise_and(shift, LANES - 1)
+    lane = lanes_of((5 * NZ, LANES))
+    near, far = lane >= rem, lane > rem
+    rest = 1.0 - frac
+
+    def place(k):
+        start = pl.multiple_of(jnp.bitwise_and(k, 1) * LANES, LANES)
+        return jnp.right_shift(k, 1), slice(None), pl.ds(start, LANES)
+
+    def turned(k):
+        tile = x_ref[place(k)]
+        return pltpu.roll(tile, rem, 1), pltpu.roll(tile, jnp.bitwise_and(rem + 1, LANES - 1), 1)
+
+    def one(k, before):
+        here = turned(k)
+        value = rest * jnp.where(near, here[0], before[0]) + frac * jnp.where(far, here[1], before[1])
+        o_ref[place(jnp.bitwise_and(k + hop, tiles - 1))] = value
+        return here
+
+    lax.fori_loop(0, tiles, one, turned(jnp.int32(tiles - 1)), unroll=2)
 
 
 def finish_kernel(y_ref, o_ref):
@@ -476,15 +503,7 @@
         out_specs=(VMEM,) * 4,
         compiler_params=PARAMS,
     )(scalars, rows, own, left, right)
-    from_below = lax.ppermute(up, "rad", [(i, i + 1) for i in range(rads - 1)])
-    from_above = lax.ppermute(dn, "rad", [(i + 1, i) for i in range(rads - 1)])
-
-    scratch = [
-        pltpu.VMEM((1, *row_shape), jnp.float32),
-        pltpu.VMEM((2, *row_shape), jnp.float32),
-        pltpu.VMEM((2, *strip_shape), jnp.float32),
-        pltpu.VMEM((2, *strip_shape), jnp.float32),
-    ]
+    scratch = loop_scratch()
 
     def inner(rows, strip):
         return pl.pallas_call(
@@ -502,27 +521,35 @@
         return pairs + [(b, a) for a, b in pairs]
 
     def moved_by(k):
-        def send(block, rows, strip):
+        def send(block, up, dn, rows, strip):
+            from_below = lax.ppermute(up, "rad", [(i, i + 1) for i in range(rads - 1)])
+            from_above = lax.ppermute(dn, "rad", [(i + 1, i) for i in range(rads - 1)])
             first, second = (lax.ppermute(block, ("az", "rad"), ends(j % azs)) for j in (k, k + 1))
-            return first, second, *inner(rows, strip)
+            seen = first[-1, :8] + second[-1, :8]
+            return first, second, from_below, from_above, seen, *inner(rows, strip)
 
         return send
 
-    first, second, updated, kept = lax.switch(hop, [moved_by(k) for k in range(azs)], end, rows, strip)
+    first, second, from_below, from_above, seen, updated, kept = lax.switch(
+        hop, [moved_by(k) for k in range(azs)], end, up, dn, rows, strip
+    )
     updated = pl.pallas_call(
         outer_kernel,
         out_shape=shape(NROW, *row_shape),
-        in_specs=[SMEM] + [VMEM] * 8,
-        out_specs=VMEM,
+        in_specs=[SMEM] + [VMEM] * 7 + [ANY] * 2,
+        out_specs=ANY,
+        input_output_aliases={9: 0},
         scratch_shapes=[
             pltpu.VMEM((2, 6, *row_shape), jnp.float32),
             pltpu.VMEM((2, 7, *row_shape), jnp.float32),
             *scratch,
+            pltpu.VMEM((2, 2, *strip_shape), jnp.float32),
             pltpu.VMEM((2, *strip_shape), jnp.float32),
-            pltpu.VMEM((2, *strip_shape), jnp.float32),
+            pltpu.VMEM((2, WIDTH, *row_shape), jnp.float32),
+            pltpu.SemaphoreType.DMA((2,)),
         ],
         compiler_params=PARAMS,
-    )(scalars, rows, strip, kept, from_below, from_above, first, second, updated)
+    )(scalars, rows, strip, kept, from_below, from_above, first, second, seen, updated)
 
     whole_row = lax.all_to_all(updated, "az", 0, 0, tiled=True)
     shifts = jnp.concatenate([shift_cells, az[None].astype(jnp.int32)])
@@ -531,7 +558,6 @@
         out_shape=shape(azs, *row_shape),
         in_specs=[SMEM, SMEM, VMEM],
         out_specs=VMEM,
-        scratch_shapes=[pltpu.VMEM(row_shape, jnp.float32)],
         compiler_params=PARAMS,
     )(shifts, shift_frac, whole_row)
     back = lax.all_to_all(moved, "az", 0, 0, tiled=True)

time: 103 us -> 96.9 us (0.941)
  Pallas kernels: 25.4 us -> 19.5 us
  starting transfers between devices: 27.6 us -> 25.4 us
    all_to_all x1, starting transfers between devices: 12.5 us -> 6.42 us  [local(): whole_row = lax.all_to_all(updated, 'az', 0, 0, tiled=True)]
    ppermute x2, starting transfers between devices: 7.8 us -> 12.9 us  [send(): lax.ppermute(block, ('az', 'rad'), ends(j % azs))]
    pallas_call x1, Pallas kernels: 10.3 us -> 7.37 us  [inner(): pl.pallas_call(inner_kernel, out_shape=(shape(NROW, *row_shape), shape(8,...]
    pallas_call x1, Pallas kernels: 3.9 us -> 2.42 us  [local(): pl.pallas_call(functools.partial(remap_kernel, azs), out_shape=shape(azs,...]
    pallas_call x1, Pallas kernels: 8.29 us -> 6.86 us  [local(): pl.pallas_call(outer_kernel, out_shape=shape(NROW, *row_shape), in_specs=...]
    ppermute x2, starting transfers between devices: 4.51 us -> 3.34 us  [the longest x1 2.06 us: send(): from_below = lax.ppermute(up, 'rad', [(i, i + 1) for i in range(rads - 1)])]
  transfers between devices with their start and end apart: 7 -> 7, of which waited for: 3 -> 4; matrix products, arithmetic and copies ran while one was open for 0% -> 1% of each run, Pallas kernels for 10% -> 8%
where the time goes in v2:
time: 96.9 us; the launch traced here: 95.8 us
  starting transfers between devices  25.4 us (26%)
  waiting for transfers between devices  24.5 us (25%)
  blocking collectives  23.1 us (24%)
  Pallas kernels  19.5 us (20%)
  local copies, waits for them, and re-layouts  1.33 us (1%)
    all_to_all x1, blocking collectives, local(): back = lax.all_to_all(moved, 'az', 0, 0, tiled=True)  23.1 us
    all_to_all x1, waiting for transfers between devices, local(): whole_row = lax.all_to_all(updated, 'az', 0, 0, tiled=True)  20.1 us
    ppermute x2, starting transfers between devices, send(): lax.ppermute(block, ('az', 'rad'), ends(j % azs))  12.9 us
    pallas_call x1, Pallas kernels, inner(): pl.pallas_call(inner_kernel, out_shape=(shape(NROW, *row_shape), shape(8,...  7.37 us
    pallas_call x1, Pallas kernels, local(): pl.pallas_call(outer_kernel, out_shape=shape(NROW, *row_shape), in_specs=...  6.86 us
    all_to_all x1, starting transfers between devices, local(): whole_row = lax.all_to_all(updated, 'az', 0, 0, tiled=True)  6.42 us
    ppermute x1, waiting for transfers between devices, local(): left = lax.ppermute(own, 'az', [(i, (i + 1) % azs) for i in range(azs)])  3.44 us
    pallas_call x1, Pallas kernels, local(): pl.pallas_call(functools.partial(remap_kernel, azs), out_shape=shape(azs,...  2.42 us
  transfers between devices with their start and end apart: 7, of which 4 were waited for; matrix products, arithmetic and copies ran while one was open for 1% of the time, Pallas kernels for 8%

profile of v2, /device:TPU:1, one launch (start us, length us, event | category | flops | bytes accessed | tf_op | source)
XLA Modules:
  0.0 95.8 jit_solution(17640283825361636850)
XLA Ops:
  0.0 0.0 copy-start
  0.0 1.3 %copy-done = f32[5,16,16,256]{3,2,1,0:T(8,128)S(1)} copy-done((f32[5,16,16,256]{3,2,1,0:T(8,128)S(1)}, f32[5,16,16,256]{3,2,1,0:T(8,128)}, u32[]{:S(2)}) %copy-start) | copy-done | bytes 1310744
  1.3 0.6 shard_map.46
  1.9 1.5 %collective-permute-start.65 = (f32[80,128]{1,0:T(8,128)S(1)}, f32[80,128]{1,0:T(8,128)S(1)}, u32[]{:S(2)}, u32[]{:S(2)}) collective-permute-start(f32[80,128]{1,0:T(8,128)S(1)} %get-tuple-element.291.own_ref), channel_id=1, source_target_pairs={{8,0},{16,8},{24,16},{32,24},{40,32},{48,40},{56,48},{64,56},{72,6... | collective-permute-start | bytes 122888 | tf_op jit(solution)/shard_map/ppermute | solution.py:497
  3.4 1.3 %collective-permute-start.64 = (f32[80,128]{1,0:T(8,128)S(1)}, f32[80,128]{1,0:T(8,128)S(1)}, u32[]{:S(2)}, u32[]{:S(2)}) collective-permute-start(f32[80,128]{1,0:T(8,128)S(1)} %get-tuple-element.291.own_ref), channel_id=1, source_target_pairs={{0,8},{8,16},{16,24},{24,32},{32,40},{40,48},{48,56},{56,64},{64,7... | collective-permute-start | bytes 122888 | tf_op jit(solution)/shard_map/ppermute | solution.py:496
  5.3 0.1 pad_add_fusion.1.rem_ref
  5.4 0.9 collective-permute-done.65.right_ref
  6.3 3.4 %collective-permute-done.64.left_ref = f32[80,128]{1,0:T(8,128)S(1)} collective-permute-done((f32[80,128]{1,0:T(8,128)S(1)}, f32[80,128]{1,0:T(8,128)S(1)}, u32[]{:S(2)}, u32[]{:S(2)}) %collective-permute-start.64) | collective-permute-done | bytes 40992 | tf_op jit(solution)/shard_map/ppermute | solution.py:496
  9.7 1.0 %shard_map.47 = (f32[80,256]{1,0:T(8,128)S(1)}, f32[7,80,128]{2,1,0:T(8,128)S(1)}, f32[7,80,128]{2,1,0:T(8,128)S(1)}, f32[7,80,128]{2,1,0:T(8,128)S(1)}) custom-call(s32[3]{0:T(128)S(1)} %pad_add_fusion.1.rem_ref, f32[16,80,256]{2,1,0:T(8,128)S(1)} %get-tuple-element.290.xt_ref, f32[80,128]{1,0:T(8,128)S(1)} %get-tuple-element.291.own_ref, ...), custom_call_target="tpu_custom_call" | custom-call | tf_op jit(solution)/shard_map/pallas_call | solution.py:499
  10.7 24.8 %conditional.1 = (f32[7,80,128]{2,1,0:T(8,128)}, f32[7,80,128]{2,1,0:T(8,128)}, f32[7,80,128]{2,1,0:T(8,128)}, f32[7,80,128]{2,1,0:T(8,128)}, f32[8,128]{1,0:T(8...) conditional(s32[]{:T(128)} %clamp.3, (f32[7,80,128]{2,1,0:T(8,128)S(1)}, ...), branch_computations={%region_0.1_spmd, %region_1.2_spmd, %region_2.3_spmd, %region_3.4_... | conditional | flops 30001024 | bytes 8794328 | solution.py:533
  10.9 8.3 %collective-permute-start.37 = (f32[7,80,128]{2,1,0:T(8,128)S(1)}, f32[7,80,128]{2,1,0:T(8,128)}, u32[]{:S(2)}, u32[]{:S(2)}) collective-permute-start(f32[7,80,128]{2,1,0:T(8,128)S(1)} %get-tuple-element.228), channel_id=1, source_target_pairs={{7,80},{15,88},{23,96},{31,104},{39,112},{47,120},{55,0},{63,8},{7... | collective-permute-start | bytes 860168 | tf_op jit(solution)/shard_map/cond/branch_9_fun/ppermute | solution.py:527
  19.3 4.6 %collective-permute-start.36 = (f32[7,80,128]{2,1,0:T(8,128)S(1)}, f32[7,80,128]{2,1,0:T(8,128)}, u32[]{:S(2)}, u32[]{:S(2)}) collective-permute-start(f32[7,80,128]{2,1,0:T(8,128)S(1)} %get-tuple-element.228), channel_id=1, source_target_pairs={{7,72},{15,80},{23,88},{31,96},{39,104},{47,112},{55,120},{63,0},{... | collective-permute-start | bytes 860168 | tf_op jit(solution)/shard_map/cond/branch_9_fun/ppermute | solution.py:527
  23.9 2.1 %collective-permute-start.38 = (f32[7,80,128]{2,1,0:T(8,128)S(1)}, f32[7,80,128]{2,1,0:T(8,128)}, u32[]{:S(2)}, u32[]{:S(2)}) collective-permute-start(f32[7,80,128]{2,1,0:T(8,128)S(1)} %get-tuple-element.229), channel_id=1, source_target_pairs={{0,1},{1,2},{2,3},{3,4},{4,5},{5,6},{6,7},{8,9},{9,10},{10,11},{11... | collective-permute-start | bytes 860168 | tf_op jit(solution)/shard_map/cond/branch_9_fun/ppermute | solution.py:525
  25.9 1.3 %collective-permute-start.39 = (f32[7,80,128]{2,1,0:T(8,128)S(1)}, f32[7,80,128]{2,1,0:T(8,128)}, u32[]{:S(2)}, u32[]{:S(2)}) collective-permute-start(f32[7,80,128]{2,1,0:T(8,128)S(1)} %get-tuple-element.230), channel_id=1, source_target_pairs={{1,0},{2,1},{3,2},{4,3},{5,4},{6,5},{7,6},{9,8},{10,9},{11,10},{12... | collective-permute-start | bytes 860168 | tf_op jit(solution)/shard_map/cond/branch_9_fun/ppermute | solution.py:526
  27.2 7.4 %branch_9_fun.1 = (f32[16,80,256]{2,1,0:T(8,128)}, f32[8,80,256]{2,1,0:T(8,128)S(1)}) custom-call(f32[16,80,256]{2,1,0:T(8,128)S(1)} %get-tuple-element.231.xt_ref, f32[80,256]{1,0:T(8,128)S(1)} %get-tuple-element.232.strip_ref), custom_call_target="tpu_custom_call" | custom-call | flops 30000000 | bytes 4194304 | tf_op jit(solution)/shard_map/cond/branch_9_fun/pallas_call | solution.py:509
  34.6 0.0 collective-permute-done.37
  34.6 0.1 collective-permute-done.36
  34.7 0.7 fusion.9
  35.4 0.0 collective-permute-done.38
  35.4 0.0 collective-permute-done.39
  35.5 6.9 %shard_map.48 = f32[16,80,256]{2,1,0:T(8,128)} custom-call(s32[3]{0:T(128)S(1)} %pad_add_fusion.1.rem_ref, f32[16,80,256]{2,1,0:T(8,128)S(1)} %get-tuple-element.290.xt_ref, f32[80,256]{1,0:T(8,128)S(1)} %get-tuple-element.292.strip_ref, f32[8,80,256]{2,1,0:T(8,128)S(1)} %get-tuple-element.296.kept_ref, ...), custom_call_target="tpu_custom_call", output_to_operand_aliasing={{}: (9, {})} | custom-call | tf_op jit(solution)/shard_map/pallas_call | solution.py:536
  42.3 0.0 copy-start.2
  42.3 0.0 copy-start.1
  42.3 6.4 %all-to-all-start = ((f32[16,80,256]{2,1,0:T(8,128)}), f32[16,80,256]{2,1,0:T(8,128)S(1)}, u32[]{:S(2)}, u32[]{:S(2)}) async-start(f32[16,80,256]{2,1,0:T(8,128)} %shard_map.48), calls=%async_computation | async-start | bytes 2621440 | tf_op jit(solution)/shard_map/all_to_all | solution.py:554
  48.8 0.0 copy-done.2
  48.8 0.1 pad_add_fusion.shift_ref
  48.8 20.1 %all-to-all-done.x_ref = f32[16,80,256]{2,1,0:T(8,128)S(1)} async-done(((f32[16,80,256]{2,1,0:T(8,128)}), f32[16,80,256]{2,1,0:T(8,128)S(1)}, u32[]{:S(2)}, u32[]{:S(2)}) %all-to-all-start) | async-done | bytes 1310752 | tf_op jit(solution)/shard_map/all_to_all | solution.py:554
  68.9 0.0 copy-done.1
  68.9 2.4 %shard_map.49 = f32[16,80,256]{2,1,0:T(8,128)S(1)} custom-call(s32[17]{0:T(128)S(1)} %pad_add_fusion.shift_ref, f32[16]{0:T(128)S(1)} %copy-done.1, f32[16,80,256]{2,1,0:T(8,128)S(1)} %all-to-all-done.x_ref), custom_call_target="tpu_custom_call" | custom-call | tf_op jit(solution)/shard_map/pallas_call | solution.py:556
  71.4 23.1 %all_to_all.10.y_ref = f32[16,80,256]{2,1,0:T(8,128)S(1)} all-to-all(f32[16,80,256]{2,1,0:T(8,128)S(1)} %shard_map.49), channel_id=1, replica_groups=mesh['az'=16,'rad'=8] {'az'}, dimensions={0} | all-to-all | bytes 2621440 | tf_op jit(solution)/shard_map/all_to_all | solution.py:563
  94.5 1.3 %shard_map.50 = f32[80,16,256]{2,1,0:T(8,128)} custom-call(f32[16,80,256]{2,1,0:T(8,128)S(1)} %all_to_all.10.y_ref), custom_call_target="tpu_custom_call" | custom-call | tf_op jit(solution)/shard_map/pallas_call | solution.py:564
Async XLA Ops:
  0.0 1.3 %copy-start = (f32[5,16,16,256]{3,2,1,0:T(8,128)S(1)}, f32[5,16,16,256]{3,2,1,0:T(8,128)}, u32[]{:S(2)}) copy-start(f32[5,16,16,256]{3,2,1,0:T(8,128)} %param.20) | copy-start | bytes 3932164
  1.9 4.4 %collective-permute-start.65 = (f32[80,128]{1,0:T(8,128)S(1)}, f32[80,128]{1,0:T(8,128)S(1)}, u32[]{:S(2)}, u32[]{:S(2)}) collective-permute-start(f32[80,128]{1,0:T(8,128)S(1)} %get-tuple-element.291.own_ref), channel_id=1, source_target_pairs={{8,0},{16,8},{24,16},{32,24},{40,32},{48,40},{56,48},{64,56},{72,6... | collective-permute-start | bytes 122888 | tf_op jit(solution)/shard_map/ppermute | solution.py:497
  3.4 6.3 %collective-permute-start.64 = (f32[80,128]{1,0:T(8,128)S(1)}, f32[80,128]{1,0:T(8,128)S(1)}, u32[]{:S(2)}, u32[]{:S(2)}) collective-permute-start(f32[80,128]{1,0:T(8,128)S(1)} %get-tuple-element.291.own_ref), channel_id=1, source_target_pairs={{0,8},{8,16},{16,24},{24,32},{32,40},{40,48},{48,56},{56,64},{64,7... | collective-permute-start | bytes 122888 | tf_op jit(solution)/shard_map/ppermute | solution.py:496
  10.9 23.7 %collective-permute-start.37 = (f32[7,80,128]{2,1,0:T(8,128)S(1)}, f32[7,80,128]{2,1,0:T(8,128)}, u32[]{:S(2)}, u32[]{:S(2)}) collective-permute-start(f32[7,80,128]{2,1,0:T(8,128)S(1)} %get-tuple-element.228), channel_id=1, source_target_pairs={{7,80},{15,88},{23,96},{31,104},{39,112},{47,120},{55,0},{63,8},{7... | collective-permute-start | bytes 860168 | tf_op jit(solution)/shard_map/cond/branch_9_fun/ppermute | solution.py:527
  19.3 15.5 %collective-permute-start.36 = (f32[7,80,128]{2,1,0:T(8,128)S(1)}, f32[7,80,128]{2,1,0:T(8,128)}, u32[]{:S(2)}, u32[]{:S(2)}) collective-permute-start(f32[7,80,128]{2,1,0:T(8,128)S(1)} %get-tuple-element.228), channel_id=1, source_target_pairs={{7,72},{15,80},{23,88},{31,96},{39,104},{47,112},{55,120},{63,0},{... | collective-permute-start | bytes 860168 | tf_op jit(solution)/shard_map/cond/branch_9_fun/ppermute | solution.py:527
  23.9 11.5 %collective-permute-start.38 = (f32[7,80,128]{2,1,0:T(8,128)S(1)}, f32[7,80,128]{2,1,0:T(8,128)}, u32[]{:S(2)}, u32[]{:S(2)}) collective-permute-start(f32[7,80,128]{2,1,0:T(8,128)S(1)} %get-tuple-element.229), channel_id=1, source_target_pairs={{0,1},{1,2},{2,3},{3,4},{4,5},{5,6},{6,7},{8,9},{9,10},{10,11},{11... | collective-permute-start | bytes 860168 | tf_op jit(solution)/shard_map/cond/branch_9_fun/ppermute | solution.py:525
  25.9 9.5 %collective-permute-start.39 = (f32[7,80,128]{2,1,0:T(8,128)S(1)}, f32[7,80,128]{2,1,0:T(8,128)}, u32[]{:S(2)}, u32[]{:S(2)}) collective-permute-start(f32[7,80,128]{2,1,0:T(8,128)S(1)} %get-tuple-element.230), channel_id=1, source_target_pairs={{1,0},{2,1},{3,2},{4,3},{5,4},{6,5},{7,6},{9,8},{10,9},{11,10},{12... | collective-permute-start | bytes 860168 | tf_op jit(solution)/shard_map/cond/branch_9_fun/ppermute | solution.py:526
  42.3 6.4 %copy-start.2 = (s32[16]{0:T(128)S(1)}, s32[16]{0:T(128)}, u32[]{:S(2)}) copy-start(s32[16]{0:T(128)} %param.21) | copy-start | bytes 196
  42.3 26.6 %copy-start.1 = (f32[16]{0:T(128)S(1)}, f32[16]{0:T(128)}, u32[]{:S(2)}) copy-start(f32[16]{0:T(128)} %frac_ref.1) | copy-start | bytes 196
  42.3 26.6 %all-to-all-start = ((f32[16,80,256]{2,1,0:T(8,128)}), f32[16,80,256]{2,1,0:T(8,128)S(1)}, u32[]{:S(2)}, u32[]{:S(2)}) async-start(f32[16,80,256]{2,1,0:T(8,128)} %shard_map.48), calls=%async_computation | async-start | bytes 2621440 | tf_op jit(solution)/shard_map/all_to_all | solution.py:554

commit v3 on v2

--- a/solution.py
+++ b/solution.py
@@ -267,24 +267,25 @@
     own_ref[...] = packed
 
 
-def rims_kernel(rem_ref, xt_ref, own_ref, left_ref, right_ref, strip_ref, up_ref, dn_ref, end_ref):
+def rims_kernel(rem_ref, xt_ref, own_ref, paired_ref, crossed_ref, strip_ref, even_ref, odd_ref, end_ref):
     lane = lanes_of((5 * NZ, LANES))
     from_low = (lane % GROUP) < GROUP // 2
     own = own_ref[...]
-    low = jnp.where(from_low, left_ref[...], own)
-    high = jnp.where(from_low, own, right_ref[...])
+    even = rem_ref[3] == 0
+    low = jnp.where(from_low, jnp.where(even, crossed_ref[...], paired_ref[...]), own)
+    high = jnp.where(from_low, own, jnp.where(even, paired_ref[...], crossed_ref[...]))
     strip_ref[:, :LANES] = low
     strip_ref[:, LANES:] = high
-    for ref, first in ((dn_ref, 0), (up_ref, NROW - WIDTH)):
+    three = WIDTH * GROUP
+    lower = jnp.where(lane < three, low, pltpu.roll(high, three, 1))
+    upper = jnp.where(lane < three, pltpu.roll(low, three, 1), pltpu.roll(high, 2 * three, 1))
+    upward = jnp.bitwise_and(rem_ref[1], 1) == 0
+    for ref, flag in ((even_ref, upward), (odd_ref, jnp.logical_not(upward))):
+        first = jnp.where(flag, NROW - WIDTH, 0)
+        ref[2 * WIDTH] = jnp.where(flag, upper, lower)
         for w in range(WIDTH):
             for side in range(2):
                 ref[2 * w + side] = xt_ref[first + w, :, side * LANES : (side + 1) * LANES]
-        three = WIDTH * GROUP
-        by = (-first * GROUP) % LANES
-        a, b = low, pltpu.roll(high, (by + three) % LANES, 1)
-        if by:
-            a = pltpu.roll(low, by, 1)
-        ref[2 * WIDTH] = jnp.where(lane < three, a, b)
 
     at_low = rem_ref[1] == 0
     first = jnp.where(at_low, 0, NROW - WIDTH)
@@ -334,7 +335,7 @@
 
 
 def outer_kernel(
-    rem_ref, xt_ref, strip_ref, kept_ref, up_ref, dn_ref, e1_ref, e2_ref, seen_ref, in_ref, whole_ref,
+    rem_ref, xt_ref, strip_ref, kept_ref, even_ref, odd_ref, e1_ref, e2_ref, seen_ref, in_ref, whole_ref,
     cons_ref, prim_ref, save_ref, first_ref, second_ref, ghost_ref, strips_ref,
     out_ref, sem,
 ):
@@ -343,10 +344,16 @@
     lane = lanes_of((5 * NZ, LANES))
     three = WIDTH * GROUP
 
-    def own_side(seg, ref):
+    upward = jnp.bitwise_and(rad, 1) == 0
+
+    def from_neighbour(seg, tile):
+        flag = upward if seg else jnp.logical_not(upward)
+        return jnp.where(flag, even_ref[tile], odd_ref[tile])
+
+    def own_side(seg):
         for w in range(WIDTH):
             for side in range(2):
-                cons_ref[seg, WIDTH * seg + w, :, side * LANES : (side + 1) * LANES] = ref[2 * w + side]
+                cons_ref[seg, WIDTH * seg + w, :, side * LANES : (side + 1) * LANES] = from_neighbour(seg, 2 * w + side)
 
     def end_side(seg, upper_ref, lower_ref, cut):
         for w in range(WIDTH):
@@ -357,9 +364,9 @@
 
     @pl.when(rad != 0)
     def _():
-        own_side(0, up_ref)
-        strips_ref[0] = up_ref[2 * WIDTH]
-        strips_ref[1] = pltpu.roll(up_ref[2 * WIDTH], LANES - three, 1)
+        own_side(0)
+        strips_ref[0] = from_neighbour(0, 2 * WIDTH)
+        strips_ref[1] = pltpu.roll(from_neighbour(0, 2 * WIDTH), LANES - three, 1)
 
     @pl.when(rad == 0)
     def _():
@@ -369,9 +376,9 @@
 
     @pl.when(rad != last)
     def _():
-        own_side(1, dn_ref)
-        strips_ref[0] = jnp.where(lane < three, strips_ref[0], pltpu.roll(dn_ref[2 * WIDTH], three, 1))
-        strips_ref[1] = jnp.where(lane < three, strips_ref[1], dn_ref[2 * WIDTH])
+        own_side(1)
+        strips_ref[0] = jnp.where(lane < three, strips_ref[0], pltpu.roll(from_neighbour(1, 2 * WIDTH), three, 1))
+        strips_ref[1] = jnp.where(lane < three, strips_ref[1], from_neighbour(1, 2 * WIDTH))
 
     @pl.when(rad == last)
     def _():
@@ -484,7 +491,7 @@
     az, rad = lax.axis_index("az"), lax.axis_index("rad")
     offset = boundary_offset[0]
     hop, rem = offset // NC, offset % NC
-    scalars = jnp.stack([rem, rad, jnp.int32(rads - 1)]).astype(jnp.int32)
+    scalars = jnp.stack([rem, rad, jnp.int32(rads - 1), az % 2]).astype(jnp.int32)
     row_shape, strip_shape = (5 * NZ, NC), (5 * NZ, LANES)
     rows, own = pl.pallas_call(
         prep_kernel,
@@ -493,16 +500,16 @@
         out_specs=(VMEM,) * 2,
         compiler_params=PARAMS,
     )(conserved.reshape(5 * NZ, NROW, NC))
-    left = lax.ppermute(own, "az", [(i, (i + 1) % azs) for i in range(azs)])
-    right = lax.ppermute(own, "az", [((i + 1) % azs, i) for i in range(azs)])
+    paired = lax.ppermute(own, "az", [(i, i ^ 1) for i in range(azs)])
+    crossed = lax.ppermute(own, "az", [(i, (i + 1 if i % 2 else i - 1) % azs) for i in range(azs)])
     rim = shape(2 * WIDTH + 1, *strip_shape)
-    strip, up, dn, end = pl.pallas_call(
+    strip, even, odd, end = pl.pallas_call(
         rims_kernel,
         out_shape=(shape(*row_shape), rim, rim, rim),
         in_specs=[SMEM] + [VMEM] * 4,
         out_specs=(VMEM,) * 4,
         compiler_params=PARAMS,
-    )(scalars, rows, own, left, right)
+    )(scalars, rows, own, paired, crossed)
     scratch = loop_scratch()
 
     def inner(rows, strip):
@@ -521,17 +528,17 @@
         return pairs + [(b, a) for a, b in pairs]
 
     def moved_by(k):
-        def send(block, up, dn, rows, strip):
-            from_below = lax.ppermute(up, "rad", [(i, i + 1) for i in range(rads - 1)])
-            from_above = lax.ppermute(dn, "rad", [(i + 1, i) for i in range(rads - 1)])
+        def send(block, even, odd, rows, strip):
+            even = lax.ppermute(even, "rad", [(i, i ^ 1) for i in range(rads)])
+            odd = lax.ppermute(odd, "rad", [(i, i + 1 if i % 2 else i - 1) for i in range(1, rads - 1)])
             first, second = (lax.ppermute(block, ("az", "rad"), ends(j % azs)) for j in (k, k + 1))
             seen = first[-1, :8] + second[-1, :8]
-            return first, second, from_below, from_above, seen, *inner(rows, strip)
+            return first, second, even, odd, seen, *inner(rows, strip)
 
         return send
 
-    first, second, from_below, from_above, seen, updated, kept = lax.switch(
-        hop, [moved_by(k) for k in range(azs)], end, up, dn, rows, strip
+    first, second, even, odd, seen, updated, kept = lax.switch(
+        hop, [moved_by(k) for k in range(azs)], end, even, odd, rows, strip
     )
     updated = pl.pallas_call(
         outer_kernel,
@@ -549,7 +556,7 @@
             pltpu.SemaphoreType.DMA((2,)),
         ],
         compiler_params=PARAMS,
-    )(scalars, rows, strip, kept, from_below, from_above, first, second, seen, updated)
+    )(scalars, rows, strip, kept, even, odd, first, second, seen, updated)
 
     whole_row = lax.all_to_all(updated, "az", 0, 0, tiled=True)
     shifts = jnp.concatenate([shift_cells, az[None].astype(jnp.int32)])

time: 96.9 us -> 94.5 us (0.975)
  waiting for transfers between devices: 24.5 us -> 21.9 us
    ppermute x4, waiting for transfers between devices: 4.3 us -> 0.12 us  [the longest x1 0.11 us: local(): paired = lax.ppermute(own, 'az', [(i, i ^ 1) for i in range(azs)])]
    ppermute x4, starting transfers between devices: 6.09 us -> 8.57 us  [the longest x1 4.41 us: local(): paired = lax.ppermute(own, 'az', [(i, i ^ 1) for i in range(azs)])]
    all_to_all x1, starting transfers between devices: 6.42 us -> 4.72 us  [local(): whole_row = lax.all_to_all(updated, 'az', 0, 0, tiled=True)]
    ppermute x2, waiting for transfers between devices: 0.14 us -> 1.63 us  [send(): lax.ppermute(block, ('az', 'rad'), ends(j % azs))]
  transfers between devices with their start and end apart: 7 -> 7, of which waited for: 4 -> 3; matrix products, arithmetic and copies ran while one was open for 1% -> 1% of each run, Pallas kernels for 8% -> 8%
where the time goes in v3:
time: 94.5 us; the launch traced here: 93.3 us
  starting transfers between devices  25.5 us (27%)
  blocking collectives  23.1 us (24%)
  waiting for transfers between devices  21.9 us (23%)
  Pallas kernels  19.5 us (21%)
  local copies, waits for them, and re-layouts  1.33 us (1%)
    all_to_all x1, blocking collectives, local(): back = lax.all_to_all(moved, 'az', 0, 0, tiled=True)  23.1 us
    all_to_all x1, waiting for transfers between devices, local(): whole_row = lax.all_to_all(updated, 'az', 0, 0, tiled=True)  20.2 us
    ppermute x2, starting transfers between devices, send(): lax.ppermute(block, ('az', 'rad'), ends(j % azs))  12.2 us
    pallas_call x1, Pallas kernels, inner(): pl.pallas_call(inner_kernel, out_shape=(shape(NROW, *row_shape), shape(8,...  7.37 us
    pallas_call x1, Pallas kernels, local(): pl.pallas_call(outer_kernel, out_shape=shape(NROW, *row_shape), in_specs=...  6.88 us
    all_to_all x1, starting transfers between devices, local(): whole_row = lax.all_to_all(updated, 'az', 0, 0, tiled=True)  4.72 us
    ppermute x1, starting transfers between devices, local(): paired = lax.ppermute(own, 'az', [(i, i ^ 1) for i in range(azs)])  4.41 us
    ppermute x1, starting transfers between devices, local(): lax.ppermute(own, 'az', [(i, (i + 1 if i % 2 else i - 1) % azs) for i in...  2.68 us
  transfers between devices with their start and end apart: 7, of which 3 were waited for; matrix products, arithmetic and copies ran while one was open for 1% of the time, Pallas kernels for 8%

profile of v3, /device:TPU:1, one launch (start us, length us, event | category | flops | bytes accessed | tf_op | source)
XLA Modules:
  0.0 93.3 jit_solution(6906399784186918986)
XLA Ops:
  0.0 0.0 copy-start
  0.0 1.3 %copy-done = f32[5,16,16,256]{3,2,1,0:T(8,128)S(1)} copy-done((f32[5,16,16,256]{3,2,1,0:T(8,128)S(1)}, f32[5,16,16,256]{3,2,1,0:T(8,128)}, u32[]{:S(2)}) %copy-start) | copy-done | bytes 1310744
  1.3 0.6 shard_map.46
  1.9 2.7 %collective-permute-start.65 = (f32[80,128]{1,0:T(8,128)S(1)}, f32[80,128]{1,0:T(8,128)S(1)}, u32[]{:S(2)}, u32[]{:S(2)}) collective-permute-start(f32[80,128]{1,0:T(8,128)S(1)} %get-tuple-element.291.own_ref), channel_id=1, source_target_pairs={{0,120},{8,16},{16,8},{24,32},{32,24},{40,48},{48,40},{56,64},{64,... | collective-permute-start | bytes 122888 | tf_op jit(solution)/shard_map/ppermute | solution.py:504
  4.6 4.4 %collective-permute-start.64 = (f32[80,128]{1,0:T(8,128)S(1)}, f32[80,128]{1,0:T(8,128)S(1)}, u32[]{:S(2)}, u32[]{:S(2)}) collective-permute-start(f32[80,128]{1,0:T(8,128)S(1)} %get-tuple-element.291.own_ref), channel_id=1, source_target_pairs={{0,8},{8,0},{16,24},{24,16},{32,40},{40,32},{48,56},{56,48},{64,72... | collective-permute-start | bytes 122888 | tf_op jit(solution)/shard_map/ppermute | solution.py:503
  9.7 0.1 pad_add_fusion.1.rem_ref
  9.8 0.0 collective-permute-done.65.crossed_ref
  9.8 0.1 collective-permute-done.64.paired_ref
  9.9 1.0 %shard_map.47 = (f32[80,256]{1,0:T(8,128)S(1)}, f32[7,80,128]{2,1,0:T(8,128)S(1)}, f32[7,80,128]{2,1,0:T(8,128)S(1)}, f32[7,80,128]{2,1,0:T(8,128)S(1)}) custom-call(s32[4]{0:T(128)S(1)} %pad_add_fusion.1.rem_ref, f32[16,80,256]{2,1,0:T(8,128)S(1)} %get-tuple-element.290.xt_ref, f32[80,128]{1,0:T(8,128)S(1)} %get-tuple-element.291.own_ref, ...), custom_call_target="tpu_custom_call" | custom-call | tf_op jit(solution)/shard_map/pallas_call | solution.py:506
  10.9 23.7 %conditional.1 = (f32[7,80,128]{2,1,0:T(8,128)}, f32[7,80,128]{2,1,0:T(8,128)}, f32[7,80,128]{2,1,0:T(8,128)}, f32[7,80,128]{2,1,0:T(8,128)}, f32[8,128]{1,0:T(8...) conditional(s32[]{:T(128)} %clamp.3, (f32[7,80,128]{2,1,0:T(8,128)S(1)}, ...), branch_computations={%region_0.1_spmd, %region_1.2_spmd, %region_2.3_spmd, %region_3.4_... | conditional | flops 30001024 | bytes 8794328 | solution.py:540
  10.9 7.2 %collective-permute-start.9 = (f32[7,80,128]{2,1,0:T(8,128)S(1)}, f32[7,80,128]{2,1,0:T(8,128)}, u32[]{:S(2)}, u32[]{:S(2)}) collective-permute-start(f32[7,80,128]{2,1,0:T(8,128)S(1)} %get-tuple-element.179), channel_id=1, source_target_pairs={{7,24},{15,32},{23,40},{31,48},{39,56},{47,64},{55,72},{63,80},{71... | collective-permute-start | bytes 860168 | tf_op jit(solution)/shard_map/cond/branch_2_fun/ppermute | solution.py:534
  18.1 5.0 %collective-permute-start.8 = (f32[7,80,128]{2,1,0:T(8,128)S(1)}, f32[7,80,128]{2,1,0:T(8,128)}, u32[]{:S(2)}, u32[]{:S(2)}) collective-permute-start(f32[7,80,128]{2,1,0:T(8,128)S(1)} %get-tuple-element.179), channel_id=1, source_target_pairs={{7,16},{15,24},{23,32},{31,40},{39,48},{47,56},{55,64},{63,72},{71... | collective-permute-start | bytes 860168 | tf_op jit(solution)/shard_map/cond/branch_2_fun/ppermute | solution.py:534
  23.1 0.1 collective-permute-start.10
  23.2 1.4 %collective-permute-start.11 = (f32[7,80,128]{2,1,0:T(8,128)S(1)}, f32[7,80,128]{2,1,0:T(8,128)}, u32[]{:S(2)}, u32[]{:S(2)}) collective-permute-start(f32[7,80,128]{2,1,0:T(8,128)S(1)} %get-tuple-element.181), channel_id=1, source_target_pairs={{1,2},{2,1},{3,4},{4,3},{5,6},{6,5},{9,10},{10,9},{11,12},{12,11},... | collective-permute-start | bytes 860168 | tf_op jit(solution)/shard_map/cond/branch_2_fun/ppermute | solution.py:533
  24.6 7.4 %branch_2_fun.1 = (f32[16,80,256]{2,1,0:T(8,128)}, f32[8,80,256]{2,1,0:T(8,128)S(1)}) custom-call(f32[16,80,256]{2,1,0:T(8,128)S(1)} %get-tuple-element.182.xt_ref, f32[80,256]{1,0:T(8,128)S(1)} %get-tuple-element.183.strip_ref), custom_call_target="tpu_custom_call" | custom-call | flops 30000000 | bytes 4194304 | tf_op jit(solution)/shard_map/cond/branch_2_fun/pallas_call | solution.py:516
  32.0 0.0 collective-permute-done.9
  32.0 1.6 %collective-permute-done.8 = f32[7,80,128]{2,1,0:T(8,128)} collective-permute-done((f32[7,80,128]{2,1,0:T(8,128)S(1)}, f32[7,80,128]{2,1,0:T(8,128)}, u32[]{:S(2)}, u32[]{:S(2)}) %collective-permute-start.8) | collective-permute-done | bytes 286752 | tf_op jit(solution)/shard_map/cond/branch_2_fun/ppermute | solution.py:534
  33.6 0.7 fusion.2
  34.3 0.0 collective-permute-done.10
  34.3 0.0 collective-permute-done.11
  34.5 6.9 %shard_map.48 = f32[16,80,256]{2,1,0:T(8,128)} custom-call(s32[4]{0:T(128)S(1)} %pad_add_fusion.1.rem_ref, f32[16,80,256]{2,1,0:T(8,128)S(1)} %get-tuple-element.290.xt_ref, f32[80,256]{1,0:T(8,128)S(1)} %get-tuple-element.292.strip_ref, f32[8,80,256]{2,1,0:T(8,128)S(1)} %get-tuple-element.296.kept_ref, ...), custom_call_target="tpu_custom_call", output_to_operand_aliasing={{}: (9, {})} | custom-call | tf_op jit(solution)/shard_map/pallas_call | solution.py:543
  41.4 0.0 copy-start.2
  41.4 0.0 copy-start.1
  41.5 4.7 %all-to-all-start = ((f32[16,80,256]{2,1,0:T(8,128)}), f32[16,80,256]{2,1,0:T(8,128)S(1)}, u32[]{:S(2)}, u32[]{:S(2)}) async-start(f32[16,80,256]{2,1,0:T(8,128)} %shard_map.48), calls=%async_computation | async-start | bytes 2621440 | tf_op jit(solution)/shard_map/all_to_all | solution.py:561
  46.2 0.0 copy-done.2
  46.2 0.1 pad_add_fusion.shift_ref
  46.3 20.2 %all-to-all-done.x_ref = f32[16,80,256]{2,1,0:T(8,128)S(1)} async-done(((f32[16,80,256]{2,1,0:T(8,128)}), f32[16,80,256]{2,1,0:T(8,128)S(1)}, u32[]{:S(2)}, u32[]{:S(2)}) %all-to-all-start) | async-done | bytes 1310752 | tf_op jit(solution)/shard_map/all_to_all | solution.py:561
  66.4 0.0 copy-done.1
  66.4 2.4 %shard_map.49 = f32[16,80,256]{2,1,0:T(8,128)S(1)} custom-call(s32[17]{0:T(128)S(1)} %pad_add_fusion.shift_ref, f32[16]{0:T(128)S(1)} %copy-done.1, f32[16,80,256]{2,1,0:T(8,128)S(1)} %all-to-all-done.x_ref), custom_call_target="tpu_custom_call" | custom-call | tf_op jit(solution)/shard_map/pallas_call | solution.py:563
  68.9 23.1 %all_to_all.10.y_ref = f32[16,80,256]{2,1,0:T(8,128)S(1)} all-to-all(f32[16,80,256]{2,1,0:T(8,128)S(1)} %shard_map.49), channel_id=1, replica_groups=mesh['az'=16,'rad'=8] {'az'}, dimensions={0} | all-to-all | bytes 2621440 | tf_op jit(solution)/shard_map/all_to_all | solution.py:570
  92.0 1.3 %shard_map.50 = f32[80,16,256]{2,1,0:T(8,128)} custom-call(f32[16,80,256]{2,1,0:T(8,128)S(1)} %all_to_all.10.y_ref), custom_call_target="tpu_custom_call" | custom-call | tf_op jit(solution)/shard_map/pallas_call | solution.py:571
Async XLA Ops:
  0.0 1.3 %copy-start = (f32[5,16,16,256]{3,2,1,0:T(8,128)S(1)}, f32[5,16,16,256]{3,2,1,0:T(8,128)}, u32[]{:S(2)}) copy-start(f32[5,16,16,256]{3,2,1,0:T(8,128)} %param.20) | copy-start | bytes 3932164
  1.9 7.9 %collective-permute-start.65 = (f32[80,128]{1,0:T(8,128)S(1)}, f32[80,128]{1,0:T(8,128)S(1)}, u32[]{:S(2)}, u32[]{:S(2)}) collective-permute-start(f32[80,128]{1,0:T(8,128)S(1)} %get-tuple-element.291.own_ref), channel_id=1, source_target_pairs={{0,120},{8,16},{16,8},{24,32},{32,24},{40,48},{48,40},{56,64},{64,... | collective-permute-start | bytes 122888 | tf_op jit(solution)/shard_map/ppermute | solution.py:504
  4.6 5.3 %collective-permute-start.64 = (f32[80,128]{1,0:T(8,128)S(1)}, f32[80,128]{1,0:T(8,128)S(1)}, u32[]{:S(2)}, u32[]{:S(2)}) collective-permute-start(f32[80,128]{1,0:T(8,128)S(1)} %get-tuple-element.291.own_ref), channel_id=1, source_target_pairs={{0,8},{8,0},{16,24},{24,16},{32,40},{40,32},{48,56},{56,48},{64,72... | collective-permute-start | bytes 122888 | tf_op jit(solution)/shard_map/ppermute | solution.py:503
  10.9 21.1 %collective-permute-start.9 = (f32[7,80,128]{2,1,0:T(8,128)S(1)}, f32[7,80,128]{2,1,0:T(8,128)}, u32[]{:S(2)}, u32[]{:S(2)}) collective-permute-start(f32[7,80,128]{2,1,0:T(8,128)S(1)} %get-tuple-element.179), channel_id=1, source_target_pairs={{7,24},{15,32},{23,40},{31,48},{39,56},{47,64},{55,72},{63,80},{71... | collective-permute-start | bytes 860168 | tf_op jit(solution)/shard_map/cond/branch_2_fun/ppermute | solution.py:534
  18.1 15.5 %collective-permute-start.8 = (f32[7,80,128]{2,1,0:T(8,128)S(1)}, f32[7,80,128]{2,1,0:T(8,128)}, u32[]{:S(2)}, u32[]{:S(2)}) collective-permute-start(f32[7,80,128]{2,1,0:T(8,128)S(1)} %get-tuple-element.179), channel_id=1, source_target_pairs={{7,16},{15,24},{23,32},{31,40},{39,48},{47,56},{55,64},{63,72},{71... | collective-permute-start | bytes 860168 | tf_op jit(solution)/shard_map/cond/branch_2_fun/ppermute | solution.py:534
  23.1 11.2 %collective-permute-start.10 = (f32[7,80,128]{2,1,0:T(8,128)S(1)}, f32[7,80,128]{2,1,0:T(8,128)}, u32[]{:S(2)}, u32[]{:S(2)}) collective-permute-start(f32[7,80,128]{2,1,0:T(8,128)S(1)} %get-tuple-element.180), channel_id=1, source_target_pairs={{0,1},{1,0},{2,3},{3,2},{4,5},{5,4},{6,7},{7,6},{8,9},{9,8},{10,11... | collective-permute-start | bytes 860168 | tf_op jit(solution)/shard_map/cond/branch_2_fun/ppermute | solution.py:532
  23.2 11.1 %collective-permute-start.11 = (f32[7,80,128]{2,1,0:T(8,128)S(1)}, f32[7,80,128]{2,1,0:T(8,128)}, u32[]{:S(2)}, u32[]{:S(2)}) collective-permute-start(f32[7,80,128]{2,1,0:T(8,128)S(1)} %get-tuple-element.181), channel_id=1, source_target_pairs={{1,2},{2,1},{3,4},{4,3},{5,6},{6,5},{9,10},{10,9},{11,12},{12,11},... | collective-permute-start | bytes 860168 | tf_op jit(solution)/shard_map/cond/branch_2_fun/ppermute | solution.py:533
  41.4 4.7 %copy-start.2 = (s32[16]{0:T(128)S(1)}, s32[16]{0:T(128)}, u32[]{:S(2)}) copy-start(s32[16]{0:T(128)} %param.21) | copy-start | bytes 196
  41.4 25.0 %copy-start.1 = (f32[16]{0:T(128)S(1)}, f32[16]{0:T(128)}, u32[]{:S(2)}) copy-start(f32[16]{0:T(128)} %frac_ref.1) | copy-start | bytes 196
  41.5 25.0 %all-to-all-start = ((f32[16,80,256]{2,1,0:T(8,128)}), f32[16,80,256]{2,1,0:T(8,128)S(1)}, u32[]{:S(2)}, u32[]{:S(2)}) async-start(f32[16,80,256]{2,1,0:T(8,128)} %shard_map.48), calls=%async_computation | async-start | bytes 2621440 | tf_op jit(solution)/shard_map/all_to_all | solution.py:561

commit v4 on v3

--- a/solution.py
+++ b/solution.py
@@ -171,33 +171,34 @@
     return lower, upper
 
 
-def predict(count, load, faces_at, sink, save_ref, unroll):
-    def state(i):
+def predict(count, tracks, unroll):
+    def state(load, i):
         cons = load(i)
         prim = primitive(cons)
         speed = sound(prim)
-        return cons, prim, speed, (flux_of(prim, cons, 1), cons, jnp.abs(prim[1]) + speed)
-
-    def keep(prim, speed, rad_state, rad):
+        return prim, speed, (flux_of(prim, cons, 1), cons, jnp.abs(prim[1]) + speed)
+
+    def keep(save_ref, prim, speed, rad_state, rad):
         put_row(save_ref, 0, rad_state[0])
         put_row(save_ref, 1, rad)
         put_row(save_ref, 2, prim)
         save_ref[3, pl.ds(0, NZ), :] = speed
         save_ref[3, pl.ds(NZ, NZ), :] = rad_state[2]
 
-    _, _, _, before = state(0)
-    _, prim, speed, here = state(1)
-    keep(prim, speed, here, twice_face(*before, *here))
-
-    def step(i, carry):
+    for load, _, _, save_ref in tracks:
+        before = state(load, 0)[2]
+        prim, speed, here = state(load, 1)
+        keep(save_ref, prim, speed, here, twice_face(*before, *here))
+
+    def one(i, load, faces_at, sink, save_ref):
         cons = load(i)
         low = row_of(save_ref, 1)
         prim = row_of(save_ref, 2)
         speed = save_ref[3, pl.ds(0, NZ), :]
         here = (row_of(save_ref, 0), cons, save_ref[3, pl.ds(NZ, NZ), :])
-        _, next_prim, next_speed, there = state(i + 1)
+        next_prim, next_speed, there = state(load, i + 1)
         rad = twice_face(*here, *there)
-        keep(next_prim, next_speed, there, rad)
+        keep(save_ref, next_prim, next_speed, there, rad)
         total = [x - y for x, y in zip(rad, low)]
         vert = first_order_faces(prim, cons, speed, 3, 0)
         total = [t + (pltpu.roll(x, NZ - 1, 0) - x) for t, x in zip(total, vert)]
@@ -208,26 +209,31 @@
             value = cons[c] - PRED * (total[c] + (upper[c] - lower[c]))
             half.append(value + 0.5 * step_ratio * source[c] if c in source else value)
         sink(i, primitive(half))
+
+    def step(i, carry):
+        for track in tracks:
+            one(i, *track)
         return carry
 
     lax.fori_loop(1, count - 1, step, 0, unroll=unroll)
 
 
-def correct(count, load, cons_at, faces_ref, group_of, sink, save_ref, unroll):
-    def sides(i):
+def correct(count, tracks, unroll):
+    def sides(load, i):
         prim = load(i)
         half_slope = [0.5 * minmod(x - a, b - x) for x, a, b in zip(prim, load(i - 1), load(i + 1))]
         return [x - s for x, s in zip(prim, half_slope)], [x + s for x, s in zip(prim, half_slope)]
 
-    _, above = sides(0)
-    high, upper_side = sides(1)
-    put_row(save_ref, 0, upper_side)
-    put_row(save_ref, 1, twice_face(*state_at(above, 1), *state_at(high, 1)))
-
-    def step(i, carry):
+    for load, *_, save_ref in tracks:
+        above = sides(load, 0)[1]
+        high, upper_side = sides(load, 1)
+        put_row(save_ref, 0, upper_side)
+        put_row(save_ref, 1, twice_face(*state_at(above, 1), *state_at(high, 1)))
+
+    def one(i, load, cons_at, faces_ref, group_of, sink, save_ref):
         below = row_of(save_ref, 0)
         low = row_of(save_ref, 1)
-        high, upper_side = sides(i + 1)
+        high, upper_side = sides(load, i + 1)
         rad = twice_face(*state_at(below, 1), *state_at(high, 1))
         put_row(save_ref, 0, upper_side)
         put_row(save_ref, 1, rad)
@@ -243,6 +249,10 @@
             value = cons[c] - CORR * (total[c] + (upper[c] - lower[c]))
             done.append(value + step_ratio * source[c] if c in source else value)
         sink(i, done)
+
+    def step(i, carry):
+        for track in tracks:
+            one(i, *track)
         return carry
 
     lax.fori_loop(1, count - 1, step, 0, unroll=unroll)
@@ -250,7 +260,7 @@
 
 def loop_scratch():
     return [
-        pltpu.VMEM((4, 5 * NZ, NC), jnp.float32),
+        pltpu.VMEM((8, 5 * NZ, NC), jnp.float32),
         pltpu.VMEM((2, 5 * NZ, LANES), jnp.float32),
         pltpu.VMEM((2, 5 * NZ, LANES), jnp.float32),
     ]
@@ -311,27 +321,25 @@
     keep_faces(first_ref, az)
     half = strip_half(cons, prim, speed, az, rolled(cons, GROUP, 1), rolled(cons, -GROUP, 1))
     keep_faces(second_ref, second_order_faces(primitive(half), 2, 1))
-    predict(
-        NROW,
+    track = (
         lambda i: row_of(xt_ref, i),
         lambda i: (first_ref, i),
         lambda i, arrays: put_row(prim_ref, i, arrays),
         save_ref,
-        2,
     )
+    predict(NROW, [track], 1)
     for n in range(4):
         kept_ref[n] = prim_ref[1 + n]
         kept_ref[4 + n] = prim_ref[NROW - 5 + n]
-    correct(
-        NROW - 4,
+    track = (
         lambda i: row_of(prim_ref, i + 2),
         lambda i: row_of(xt_ref, i + 2),
         second_ref,
         lambda i: i + 2,
         lambda i, arrays: put_row(out_ref, i + 2, arrays),
         save_ref,
-        2,
     )
+    correct(NROW - 4, [track], 2)
 
 
 def outer_kernel(
@@ -418,28 +426,26 @@
         ghost_ref[0, side] = jnp.where(group == 3, pltpu.roll(mine, 3 * GROUP, 1), both)
         ghost_ref[1, side] = jnp.where(group == 1, pltpu.roll(mine, 2 * GROUP, 1), pltpu.roll(both, LANES - GROUP, 1))
 
-    def segment(seg, carry):
-        predict(
-            5,
+    def predicted(seg):
+        return (
             lambda i: row_of(cons_ref, seg, i + seg),
             lambda i: (ghost_ref.at[seg], i),
             lambda i, arrays: put_row(prim_ref.at[seg], i - 1 + 4 * seg, arrays),
-            save_ref,
-            1,
+            save_ref.at[pl.ds(4 * seg, 4)],
         )
-        correct(
-            5,
+
+    def corrected(seg):
+        return (
             lambda i: row_of(prim_ref, seg, i + 1),
             lambda i: row_of(cons_ref, seg, i + 2 - 3 * seg),
             second_ref,
             lambda i: i - 1 + 13 * seg,
             lambda i, arrays: put_row(out_ref.at[seg], i - 1, arrays),
-            save_ref,
-            1,
+            save_ref.at[pl.ds(4 * seg, 4)],
         )
-        return carry
-
-    lax.fori_loop(0, 2, segment, 0)
+
+    predict(5, [predicted(0), predicted(1)], 1)
+    correct(5, [corrected(0), corrected(1)], 1)
     copies = [
         pltpu.make_async_copy(out_ref.at[seg], whole_ref.at[pl.ds(seg * (NROW - WIDTH), WIDTH)], sem.at[seg])
         for seg in range(2)
@@ -450,9 +456,8 @@
         copy.wait()
 
 
-def remap_kernel(count, shift_ref, frac_ref, x_ref, o_ref):
-    row = shift_ref[NROW]
-    shift, frac = shift_ref[row], frac_ref[row]
+def remap_kernel(count, turn_ref, x_ref, o_ref):
+    shift, frac = turn_ref[0].astype(jnp.int32), turn_ref[1]
     tiles = 2 * count
     hop = jnp.bitwise_and(jnp.right_shift(shift, 7), tiles - 1)
     rem = jnp.bitwise_and(shift, LANES - 1)
@@ -510,6 +515,11 @@
         out_specs=(VMEM,) * 4,
         compiler_params=PARAMS,
     )(scalars, rows, own, paired, crossed)
+    row_shift = lax.dynamic_slice_in_dim(shift_cells, az, 1)
+    row_frac = lax.dynamic_slice_in_dim(shift_frac, az, 1)
+    turn = jnp.concatenate([row_shift.astype(jnp.float32), row_frac])
+    strip, turn = lax.optimization_barrier((strip, turn))
+
     scratch = loop_scratch()
 
     def inner(rows, strip):
@@ -559,14 +569,13 @@
     )(scalars, rows, strip, kept, even, odd, first, second, seen, updated)
 
     whole_row = lax.all_to_all(updated, "az", 0, 0, tiled=True)
-    shifts = jnp.concatenate([shift_cells, az[None].astype(jnp.int32)])
     moved = pl.pallas_call(
         functools.partial(remap_kernel, azs),
         out_shape=shape(azs, *row_shape),
-        in_specs=[SMEM, SMEM, VMEM],
+        in_specs=[SMEM, VMEM],
         out_specs=VMEM,
         compiler_params=PARAMS,
-    )(shifts, shift_frac, whole_row)
+    )(turn, whole_row)
     back = lax.all_to_all(moved, "az", 0, 0, tiled=True)
     result = pl.pallas_call(
         finish_kernel,

time: 94.5 us -> 92.5 us (0.979)
  blocking collectives: 23.1 us -> 48.1 us
  waiting for transfers between devices: 21.9 us -> 4.44 us
  starting transfers between devices: 25.5 us -> 15.5 us
  Pallas kernels: 19.5 us -> 17.7 us
  local copies, waits for them, and re-layouts: 1.33 us -> 2.58 us
    all_to_all x0 -> x1, blocking collectives: none -> 24.9 us  [local(): whole_row = lax.all_to_all(updated, 'az', 0, 0, tiled=True)]
    all_to_all x1 -> x0, waiting for transfers between devices: 20.2 us -> none  [local(): whole_row = lax.all_to_all(updated, 'az', 0, 0, tiled=True)]
    ppermute x2, starting transfers between devices: 12.2 us -> 6.95 us  [send(): lax.ppermute(block, ('az', 'rad'), ends(j % azs))]
    all_to_all x1 -> x0, starting transfers between devices: 4.72 us -> none  [local(): whole_row = lax.all_to_all(updated, 'az', 0, 0, tiled=True)]
    ppermute x2, waiting for transfers between devices: 1.63 us -> 4.43 us  [send(): lax.ppermute(block, ('az', 'rad'), ends(j % azs))]
    dynamic_slice x0 -> x2, local copies, waits for them, and re-layouts: none -> 1.23 us  [the longest x1 0.64 us: local(): row_shift = lax.dynamic_slice_in_dim(shift_cells, az, 1)]
    pallas_call x1, Pallas kernels: 6.88 us -> 5.79 us  [local(): pl.pallas_call(outer_kernel, out_shape=shape(NROW, *row_shape), in_specs=...]
  transfers between devices with their start and end apart: 7 -> 6, of which waited for: 3 -> 1; matrix products, arithmetic and copies ran while one was open for 1% -> 3% of each run, Pallas kernels for 8% -> 7%
where the time goes in v4:
time: 92.5 us; the launch traced here: 92 us
  blocking collectives  48.1 us (52%)
  Pallas kernels  17.7 us (19%)
  starting transfers between devices  15.5 us (17%)
  waiting for transfers between devices  4.44 us (5%)
  local copies, waits for them, and re-layouts  2.58 us (3%)
  other arithmetic  1.48 us (2%)
  between operations  1.37 us (1%)
    all_to_all x1, blocking collectives, local(): whole_row = lax.all_to_all(updated, 'az', 0, 0, tiled=True)  24.9 us
    all_to_all x1, blocking collectives, local(): back = lax.all_to_all(moved, 'az', 0, 0, tiled=True)  23.2 us
    ppermute x2, starting transfers between devices, send(): lax.ppermute(block, ('az', 'rad'), ends(j % azs))  6.95 us
    pallas_call x1, Pallas kernels, inner(): pl.pallas_call(inner_kernel, out_shape=(shape(NROW, *row_shape), shape(8,...  6.69 us
    pallas_call x1, Pallas kernels, local(): pl.pallas_call(outer_kernel, out_shape=shape(NROW, *row_shape), in_specs=...  5.79 us
    ppermute x2, waiting for transfers between devices, send(): lax.ppermute(block, ('az', 'rad'), ends(j % azs))  4.43 us
    ppermute x1, starting transfers between devices, local(): paired = lax.ppermute(own, 'az', [(i, i ^ 1) for i in range(azs)])  4.41 us
    ppermute x1, starting transfers between devices, local(): lax.ppermute(own, 'az', [(i, (i + 1 if i % 2 else i - 1) % azs) for i in...  2.68 us
  transfers between devices with their start and end apart: 6, of which 1 were waited for; matrix products, arithmetic and copies ran while one was open for 3% of the time, Pallas kernels for 7%

profile of v4, /device:TPU:1, one launch (start us, length us, event | category | flops | bytes accessed | tf_op | source)
XLA Modules:
  0.0 92.0 jit_solution(1158915457627337238)
XLA Ops:
  0.0 0.0 copy-start.1
  0.0 0.0 copy-start.2
  0.0 0.0 copy-start
  0.0 1.3 %copy-done = f32[5,16,16,256]{3,2,1,0:T(8,128)S(1)} copy-done((f32[5,16,16,256]{3,2,1,0:T(8,128)S(1)}, f32[5,16,16,256]{3,2,1,0:T(8,128)}, u32[]{:S(2)}) %copy-start) | copy-done | bytes 1310744
  1.3 0.6 shard_map.46
  1.9 2.7 %collective-permute-start.65 = (f32[80,128]{1,0:T(8,128)S(1)}, f32[80,128]{1,0:T(8,128)S(1)}, u32[]{:S(2)}, u32[]{:S(2)}) collective-permute-start(f32[80,128]{1,0:T(8,128)S(1)} %get-tuple-element.293.own_ref), channel_id=1, source_target_pairs={{0,120},{8,16},{16,8},{24,32},{32,24},{40,48},{48,40},{56,64},{64,... | collective-permute-start | bytes 122888 | tf_op jit(solution)/shard_map/ppermute | solution.py:509
  4.6 4.4 %collective-permute-start.64 = (f32[80,128]{1,0:T(8,128)S(1)}, f32[80,128]{1,0:T(8,128)S(1)}, u32[]{:S(2)}, u32[]{:S(2)}) collective-permute-start(f32[80,128]{1,0:T(8,128)S(1)} %get-tuple-element.293.own_ref), channel_id=1, source_target_pairs={{0,8},{8,0},{16,24},{24,16},{32,40},{40,32},{48,56},{56,48},{64,72... | collective-permute-start | bytes 122888 | tf_op jit(solution)/shard_map/ppermute | solution.py:508
  9.7 0.0 copy-done.1
  9.7 0.6 dynamic_slice.7
  10.3 0.0 copy-done.2
  10.3 0.6 dynamic_slice.6
  11.6 0.7 pad_maximum_fusion.turn_ref
  12.3 0.1 pad_add_fusion.rem_ref
  12.4 0.0 collective-permute-done.65.crossed_ref
  12.4 0.0 collective-permute-done.64.paired_ref
  12.4 1.0 %shard_map.47 = (f32[80,256]{1,0:T(8,128)S(1)}, f32[7,80,128]{2,1,0:T(8,128)S(1)}, f32[7,80,128]{2,1,0:T(8,128)S(1)}, f32[7,80,128]{2,1,0:T(8,128)S(1)}) custom-call(s32[4]{0:T(128)S(1)} %pad_add_fusion.rem_ref, f32[16,80,256]{2,1,0:T(8,128)S(1)} %get-tuple-element.292.xt_ref, f32[80,128]{1,0:T(8,128)S(1)} %get-tuple-element.293.own_ref, ...), custom_call_target="tpu_custom_call" | custom-call | tf_op jit(solution)/shard_map/pallas_call | solution.py:511
  13.4 21.0 %conditional.1 = (f32[7,80,128]{2,1,0:T(8,128)}, f32[7,80,128]{2,1,0:T(8,128)}, f32[7,80,128]{2,1,0:T(8,128)}, f32[7,80,128]{2,1,0:T(8,128)}, f32[8,128]{1,0:T(8...) conditional(s32[]{:T(128)} %clamp.3, ...), branch_computations={%region_0.1_spmd, %region_1.2_spmd, %region_2.3_spmd, %region_3.4_... | conditional | flops 30001024 | bytes 8794328 | solution.py:550
  13.6 5.0 %collective-permute-start.25 = (f32[7,80,128]{2,1,0:T(8,128)S(1)}, f32[7,80,128]{2,1,0:T(8,128)}, u32[]{:S(2)}, u32[]{:S(2)}) collective-permute-start(f32[7,80,128]{2,1,0:T(8,128)S(1)} %get-tuple-element.207), channel_id=1, source_target_pairs={{7,56},{15,64},{23,72},{31,80},{39,88},{47,96},{55,104},{63,112},{... | collective-permute-start | bytes 860168 | tf_op jit(solution)/shard_map/cond/branch_6_fun/ppermute | solution.py:544
  18.6 1.9 %collective-permute-start.24 = (f32[7,80,128]{2,1,0:T(8,128)S(1)}, f32[7,80,128]{2,1,0:T(8,128)}, u32[]{:S(2)}, u32[]{:S(2)}) collective-permute-start(f32[7,80,128]{2,1,0:T(8,128)S(1)} %get-tuple-element.207), channel_id=1, source_target_pairs={{7,48},{15,56},{23,64},{31,72},{39,80},{47,88},{55,96},{63,104},{7... | collective-permute-start | bytes 860168 | tf_op jit(solution)/shard_map/cond/branch_6_fun/ppermute | solution.py:544
  20.6 0.1 collective-permute-start.26
  20.7 1.4 %collective-permute-start.27 = (f32[7,80,128]{2,1,0:T(8,128)S(1)}, f32[7,80,128]{2,1,0:T(8,128)}, u32[]{:S(2)}, u32[]{:S(2)}) collective-permute-start(f32[7,80,128]{2,1,0:T(8,128)S(1)} %get-tuple-element.209), channel_id=1, source_target_pairs={{1,2},{2,1},{3,4},{4,3},{5,6},{6,5},{9,10},{10,9},{11,12},{12,11},... | collective-permute-start | bytes 860168 | tf_op jit(solution)/shard_map/cond/branch_6_fun/ppermute | solution.py:543
  22.0 6.7 %branch_6_fun.1 = (f32[16,80,256]{2,1,0:T(8,128)S(1)}, f32[8,80,256]{2,1,0:T(8,128)S(1)}) custom-call(f32[16,80,256]{2,1,0:T(8,128)S(1)} %get-tuple-element.210.xt_ref, f32[80,256]{1,0:T(8,128)S(1)} %get-tuple-element.211.strip_ref), custom_call_target="tpu_custom_call" | custom-call | flops 30000000 | bytes 4194304 | tf_op jit(solution)/shard_map/cond/branch_6_fun/pallas_call | solution.py:526
  28.7 0.0 collective-permute-done.25
  28.8 4.4 %collective-permute-done.24 = f32[7,80,128]{2,1,0:T(8,128)} collective-permute-done((f32[7,80,128]{2,1,0:T(8,128)S(1)}, f32[7,80,128]{2,1,0:T(8,128)}, u32[]{:S(2)}, u32[]{:S(2)}) %collective-permute-start.24) | collective-permute-done | bytes 286752 | tf_op jit(solution)/shard_map/cond/branch_6_fun/ppermute | solution.py:544
  33.2 0.7 fusion.6
  33.9 0.0 collective-permute-done.26
  33.9 0.0 collective-permute-done.27
  34.4 5.8 %shard_map.48 = f32[16,80,256]{2,1,0:T(8,128)S(1)} custom-call(s32[4]{0:T(128)S(1)} %pad_add_fusion.rem_ref, f32[16,80,256]{2,1,0:T(8,128)S(1)} %get-tuple-element.292.xt_ref, f32[80,256]{1,0:T(8,128)S(1)} %get-tuple-element.296.strip_ref, f32[8,80,256]{2,1,0:T(8,128)S(1)} %get-tuple-element.300.kept_ref, ...), custom_call_target="tpu_custom_call", output_to_operand_aliasing={{}: (9, {})} | custom-call | tf_op jit(solution)/shard_map/pallas_call | solution.py:553
  40.2 24.9 %all_to_all.10.x_ref = f32[16,80,256]{2,1,0:T(8,128)S(1)} all-to-all(f32[16,80,256]{2,1,0:T(8,128)S(1)} %shard_map.48), channel_id=1, replica_groups=mesh['az'=16,'rad'=8] {'az'}, dimensions={0} | all-to-all | bytes 2621440 | tf_op jit(solution)/shard_map/all_to_all | solution.py:571
  65.1 2.4 %shard_map.49 = f32[16,80,256]{2,1,0:T(8,128)S(1)} custom-call(f32[2]{0:T(128)S(1)} %pad_maximum_fusion.turn_ref, f32[16,80,256]{2,1,0:T(8,128)S(1)} %all_to_all.10.x_ref), custom_call_target="tpu_custom_call" | custom-call | tf_op jit(solution)/shard_map/pallas_call | solution.py:572
  67.5 23.2 %all_to_all.11.y_ref = f32[16,80,256]{2,1,0:T(8,128)S(1)} all-to-all(f32[16,80,256]{2,1,0:T(8,128)S(1)} %shard_map.49), channel_id=1, replica_groups=mesh['az'=16,'rad'=8] {'az'}, dimensions={0} | all-to-all | bytes 2621440 | tf_op jit(solution)/shard_map/all_to_all | solution.py:579
  90.7 1.3 %shard_map.50 = f32[80,16,256]{2,1,0:T(8,128)} custom-call(f32[16,80,256]{2,1,0:T(8,128)S(1)} %all_to_all.11.y_ref), custom_call_target="tpu_custom_call" | custom-call | tf_op jit(solution)/shard_map/pallas_call | solution.py:580
Async XLA Ops:
  0.0 9.7 %copy-start.1 = (f32[16]{0:T(128)S(1)}, f32[16]{0:T(128)}, u32[]{:S(2)}) copy-start(f32[16]{0:T(128)} %param.22) | copy-start | bytes 196
  0.0 10.3 %copy-start.2 = (s32[16]{0:T(128)S(1)}, s32[16]{0:T(128)}, u32[]{:S(2)}) copy-start(s32[16]{0:T(128)} %param.21) | copy-start | bytes 196
  0.0 1.3 %copy-start = (f32[5,16,16,256]{3,2,1,0:T(8,128)S(1)}, f32[5,16,16,256]{3,2,1,0:T(8,128)}, u32[]{:S(2)}) copy-start(f32[5,16,16,256]{3,2,1,0:T(8,128)} %param.20) | copy-start | bytes 3932164
  1.9 10.5 %collective-permute-start.65 = (f32[80,128]{1,0:T(8,128)S(1)}, f32[80,128]{1,0:T(8,128)S(1)}, u32[]{:S(2)}, u32[]{:S(2)}) collective-permute-start(f32[80,128]{1,0:T(8,128)S(1)} %get-tuple-element.293.own_ref), channel_id=1, source_target_pairs={{0,120},{8,16},{16,8},{24,32},{32,24},{40,48},{48,40},{56,64},{64,... | collective-permute-start | bytes 122888 | tf_op jit(solution)/shard_map/ppermute | solution.py:509
  4.6 7.8 %collective-permute-start.64 = (f32[80,128]{1,0:T(8,128)S(1)}, f32[80,128]{1,0:T(8,128)S(1)}, u32[]{:S(2)}, u32[]{:S(2)}) collective-permute-start(f32[80,128]{1,0:T(8,128)S(1)} %get-tuple-element.293.own_ref), channel_id=1, source_target_pairs={{0,8},{8,0},{16,24},{24,16},{32,40},{40,32},{48,56},{56,48},{64,72... | collective-permute-start | bytes 122888 | tf_op jit(solution)/shard_map/ppermute | solution.py:508
  13.6 15.1 %collective-permute-start.25 = (f32[7,80,128]{2,1,0:T(8,128)S(1)}, f32[7,80,128]{2,1,0:T(8,128)}, u32[]{:S(2)}, u32[]{:S(2)}) collective-permute-start(f32[7,80,128]{2,1,0:T(8,128)S(1)} %get-tuple-element.207), channel_id=1, source_target_pairs={{7,56},{15,64},{23,72},{31,80},{39,88},{47,96},{55,104},{63,112},{... | collective-permute-start | bytes 860168 | tf_op jit(solution)/shard_map/cond/branch_6_fun/ppermute | solution.py:544
  18.6 14.5 %collective-permute-start.24 = (f32[7,80,128]{2,1,0:T(8,128)S(1)}, f32[7,80,128]{2,1,0:T(8,128)}, u32[]{:S(2)}, u32[]{:S(2)}) collective-permute-start(f32[7,80,128]{2,1,0:T(8,128)S(1)} %get-tuple-element.207), channel_id=1, source_target_pairs={{7,48},{15,56},{23,64},{31,72},{39,80},{47,88},{55,96},{63,104},{7... | collective-permute-start | bytes 860168 | tf_op jit(solution)/shard_map/cond/branch_6_fun/ppermute | solution.py:544
  20.6 13.3 %collective-permute-start.26 = (f32[7,80,128]{2,1,0:T(8,128)S(1)}, f32[7,80,128]{2,1,0:T(8,128)}, u32[]{:S(2)}, u32[]{:S(2)}) collective-permute-start(f32[7,80,128]{2,1,0:T(8,128)S(1)} %get-tuple-element.208), channel_id=1, source_target_pairs={{0,1},{1,0},{2,3},{3,2},{4,5},{5,4},{6,7},{7,6},{8,9},{9,8},{10,11... | collective-permute-start | bytes 860168 | tf_op jit(solution)/shard_map/cond/branch_6_fun/ppermute | solution.py:542
  20.7 13.2 %collective-permute-start.27 = (f32[7,80,128]{2,1,0:T(8,128)S(1)}, f32[7,80,128]{2,1,0:T(8,128)}, u32[]{:S(2)}, u32[]{:S(2)}) collective-permute-start(f32[7,80,128]{2,1,0:T(8,128)S(1)} %get-tuple-element.209), channel_id=1, source_target_pairs={{1,2},{2,1},{3,4},{4,3},{5,6},{6,5},{9,10},{10,9},{11,12},{12,11},... | collective-permute-start | bytes 860168 | tf_op jit(solution)/shard_map/cond/branch_6_fun/ppermute | solution.py:543
